TPU v7x, 256 devices: a whole 4x4x8 slice. The times are simulated.
256 devices in a mesh: segment: 4 (over x_lo, core), lat: 16 (over z, x_hi), lon: 4 (over y).
Axes of the slice: x: 4 (x_hi: 2, x_lo: 2; x = x_hi * 2 + x_lo), y: 4, z: 8, core: 2. Of those that a mesh axis runs over, the one named last changes fastest.
Arguments:
- fields: bfloat16 [4, 192, 24, 512], P(None, 'lat', 'lon'), may hold values from -6 to 6
- cotangent: bfloat16 [4, 192, 24, 512], P(None, 'lat', 'lon'), may hold values from -6 to 6
- depths: int32 [4], P('segment'), may hold values from 1 to 2, as said below
- w_qkv: bfloat16 [4, 2, 512, 1536], P('segment'), may hold values from -0.25 to 0.25
- w_out: bfloat16 [4, 2, 512, 512], P('segment'), may hold values from -0.25 to 0.25
Outputs:
- segment_out: bfloat16 [4, 4, 192, 24, 512], P('segment', None, 'lat', 'lon')
- segment_grad: float32 [4, 4, 192, 24, 512], P('segment', None, 'lat', 'lon')
- qkv_grad: float32 [4, 2, 512, 1536], P('segment', None, ('lat', 'lon'))
- out_grad: float32 [4, 2, 512, 512], P('segment', None, ('lat', 'lon'))
Inputs may be any that keep to these rules, and one draw needn't show every extreme that they name: Each section runs its first depths layers; some section runs all 2 layers and some only one.
All inputs are finite; a program needn't handle non-finite values.
Results may differ from a plain program's by a relative error of at most 0.028.
Values may be sent and summed in bfloat16 or wider, within the bound.
A program may use at most 192 MiB of HBM per device.

v0:
```python
from functools import partial

import jax
import jax.numpy as jnp
from jax import lax
from jax.sharding import PartitionSpec as P

HEADS = 8
HS = 64
WIN_LEV = 2
WIN_LON = 6
MICRO = 2
MAXL = 2


EPSILON = 1e-05


def padded_2(cells, sides, width):
    for axis, dim in sides:
        count = lax.axis_size(axis)
        ends = count - 1
        head = lax.slice_in_dim(cells, 0, width, axis=dim)
        tail = lax.slice_in_dim(cells, cells.shape[dim] - width, cells.shape[dim], axis=dim)
        cells = jnp.concatenate(
            [
                lax.ppermute(tail, axis, [(i, (i + 1) % count) for i in range(ends)]),
                cells,
                lax.ppermute(head, axis, [((i + 1) % count, i) for i in range(ends)]),
            ],
            axis=dim,
        )
    return cells


def passed_along(value, axis, steps):
    count = lax.axis_size(axis)
    leading, last = (max(0, -steps), min(count, count - steps))
    return lax.ppermute(value, axis, [(source, source + steps) for source in range(leading, last)])


def for_sending(value):
    return jax.tree.map(lambda a: a.astype(jnp.bfloat16) if a.dtype == jnp.float32 else a, value)


def normalize(stream):
    center = stream - jnp.mean(stream, axis=-1, keepdims=True)
    inverse = lax.rsqrt(jnp.mean(center * center, axis=-1, keepdims=True) + EPSILON)
    return (center * inverse, inverse)


def norm_back(scaled, inverse, gradient):
    middle = gradient - jnp.mean(gradient, axis=-1, keepdims=True)
    return inverse * (middle - scaled * jnp.mean(gradient * scaled, axis=-1, keepdims=True))


def project(inputs, weight):
    flattened = inputs.reshape(-1, inputs.shape[-1])
    result = jnp.dot(flattened, weight, preferred_element_type=jnp.float32)
    return result.reshape(inputs.shape[:-1] + (weight.shape[-1],))


def project_back(inputs, weight):
    flattened = inputs.reshape(-1, inputs.shape[-1])
    result = lax.dot_general(
        flattened, weight, (((1,), (1,)), ((), ())), preferred_element_type=jnp.float32
    )
    return result.reshape(inputs.shape[:-1] + (weight.shape[0],))


def transpose_dot(left_rows, right_rows):
    left_flat = left_rows.reshape(-1, left_rows.shape[-1])
    right_flat = right_rows.reshape(-1, right_rows.shape[-1])
    return lax.dot_general(
        left_flat, right_flat, (((0,), (0,)), ((), ())), preferred_element_type=jnp.float32
    )


def to_windows(field, height):
    level_count, band_rows, strip_cols, channels = field.shape
    shaped = field.reshape(
        level_count // WIN_LEV,
        WIN_LEV,
        band_rows // height,
        height,
        strip_cols // WIN_LON,
        WIN_LON,
        channels,
    )
    shaped = shaped.transpose(0, 2, 4, 1, 3, 5, 6)
    return shaped.reshape(-1, WIN_LEV * height * WIN_LON, channels)


def from_windows(windows, level_count, band_rows, strip_cols, height):
    channels = windows.shape[-1]
    shaped = windows.reshape(
        level_count // WIN_LEV,
        band_rows // height,
        strip_cols // WIN_LON,
        WIN_LEV,
        height,
        WIN_LON,
        channels,
    )
    shaped = shaped.transpose(0, 3, 1, 4, 2, 5, 6)
    return shaped.reshape(level_count, band_rows, strip_cols, channels)


def attend(queries, key_rows, key_valid, w_qkv, w_out):
    model_width = queries.shape[-1]
    queried = project(queries, w_qkv[:, :model_width]).astype(jnp.bfloat16)
    keyvals = project(key_rows, w_qkv[:, model_width:]).astype(jnp.bfloat16)
    qheads = queried.reshape(queried.shape[:2] + (HEADS, HS))
    kheads = keyvals[..., :model_width].reshape(keyvals.shape[:2] + (HEADS, HS))
    vheads = keyvals[..., model_width:].reshape(keyvals.shape[:2] + (HEADS, HS))
    score_scale = HS ** (-0.5)
    scores = (
        jnp.einsum("bqhe,bkhe->bhqk", qheads, kheads, preferred_element_type=jnp.float32)
        * score_scale
    )
    exponent = jnp.exp(scores) * key_valid[:, None, None, :]
    attn_probs = exponent / jnp.sum(exponent, axis=-1, keepdims=True)
    probs_low = attn_probs.astype(jnp.bfloat16)
    mixed = jnp.einsum("bhqk,bkhe->bqhe", probs_low, vheads, preferred_element_type=jnp.float32)
    mixed_low = mixed.reshape(queried.shape).astype(jnp.bfloat16)
    branch = project(mixed_low, w_out)
    return (branch, (qheads, kheads, vheads, attn_probs, probs_low, mixed_low))


def attend_back(gradient, stored, w_out):
    qheads, kheads, vheads, attn_probs, probs_low, mixed_low = stored
    model_width = w_out.shape[0]
    score_scale = HS ** (-0.5)
    grad_low = gradient.astype(jnp.bfloat16)
    grad_mixed = project_back(grad_low, w_out).astype(jnp.bfloat16).reshape(qheads.shape)
    grad_probs = jnp.einsum(
        "bqhe,bkhe->bhqk", grad_mixed, vheads, preferred_element_type=jnp.float32
    )
    grad_values = jnp.einsum(
        "bhqk,bqhe->bkhe", probs_low, grad_mixed, preferred_element_type=jnp.float32
    )
    inner = jnp.sum(attn_probs * grad_probs, axis=-1, keepdims=True)
    grad_scores = (attn_probs * (grad_probs - inner) * score_scale).astype(jnp.bfloat16)
    grad_query = jnp.einsum(
        "bhqk,bkhe->bqhe", grad_scores, kheads, preferred_element_type=jnp.float32
    )
    grad_keys = jnp.einsum(
        "bhqk,bqhe->bkhe", grad_scores, qheads, preferred_element_type=jnp.float32
    )
    grad_query = grad_query.reshape(grad_query.shape[:2] + (model_width,))
    grad_pairs = jnp.concatenate(
        [
            grad_keys.reshape(grad_keys.shape[:2] + (model_width,)),
            grad_values.reshape(grad_values.shape[:2] + (model_width,)),
        ],
        axis=-1,
    )
    out_rows = (mixed_low.reshape(-1, model_width), grad_low.reshape(-1, model_width))
    return (out_rows, grad_query, grad_pairs)


def finish(row_source, grad_query, grad_pairs, w_qkv):
    model_width = row_source.shape[-1]
    query_low = grad_query.astype(jnp.bfloat16)
    pairs_low = grad_pairs.astype(jnp.bfloat16)
    part_query = project_back(query_low, w_qkv[:, :model_width])
    part_keys = project_back(pairs_low, w_qkv[:, model_width:])
    joined = jnp.concatenate([query_low, pairs_low], axis=-1)
    qkv_rows = (row_source.reshape(-1, model_width), joined.reshape(-1, 3 * model_width))
    return (qkv_rows, part_query, part_keys)


def layer_forward(stream, sublayer, active, w_qkv, w_out, plain_valid, shifted_valid):
    level_count, band_rows, strip_cols, model_width = stream.shape
    half_rows = band_rows // 2
    scaled, inverse = normalize(stream)
    normed = scaled.astype(jnp.bfloat16)
    if sublayer % 2 == 0:
        key_rows = to_windows(normed, band_rows)
        branch, stored = attend(key_rows, key_rows, plain_valid, w_qkv, w_out)
        branch = from_windows(branch, level_count, band_rows, strip_cols, band_rows)
    else:
        padded = padded_2(normed, (("lat", 1),), half_rows)
        key_rows = to_windows(padded, band_rows)
        queries = to_windows(normed, half_rows)
        branch, stored = attend(queries, key_rows, shifted_valid, w_qkv, w_out)
        branch = from_windows(branch, level_count, band_rows, strip_cols, half_rows)
    return (stream + active * branch, (scaled, inverse, normed, key_rows, stored))


def layer_backward(gradient, kept_state, sublayer, active, w_qkv, w_out):
    scaled, inverse, normed, key_rows, stored = kept_state
    level_count, band_rows, strip_cols, model_width = gradient.shape
    half_rows = band_rows // 2
    branch_grad = gradient * active
    if sublayer % 2 == 0:
        windowed = to_windows(branch_grad, band_rows)
        out_rows, grad_query, grad_pairs = attend_back(windowed, stored, w_out)
        qkv_rows, part_query, part_keys = finish(key_rows, grad_query, grad_pairs, w_qkv)
        grad_normed = from_windows(
            part_query + part_keys, level_count, band_rows, strip_cols, band_rows
        )
    else:
        windowed = to_windows(branch_grad, half_rows)
        out_rows, grad_query, grad_pairs = attend_back(windowed, stored, w_out)
        query_field = from_windows(grad_query, level_count, band_rows, strip_cols, half_rows)
        pair_field = from_windows(
            grad_pairs, level_count, band_rows + 2 * half_rows, strip_cols, band_rows
        )
        rim_grads = jnp.concatenate(
            [pair_field[:, :half_rows], pair_field[:, half_rows + band_rows :]], axis=1
        )
        beside_all = padded_2(rim_grads.astype(jnp.bfloat16), (("lat", 1),), half_rows).astype(
            rim_grads.dtype
        )
        own_pairs = pair_field[:, half_rows : half_rows + band_rows] + jnp.concatenate(
            [beside_all[:, :half_rows], beside_all[:, -half_rows:]], axis=1
        )
        qkv_rows, part_query, part_keys = finish(normed, query_field, own_pairs, w_qkv)
        grad_normed = part_query + part_keys
    return (gradient + norm_back(scaled, inverse, grad_normed), qkv_rows, out_rows)


def stack_all(*pieces):
    return jnp.stack(pieces)


def local(fields, cotangent, depths, w_qkv, w_out):
    segment_at = lax.axis_index("segment")
    last_segment = lax.axis_size("segment") - 1
    lat_at = lax.axis_index("lat")
    lat_total = lax.axis_size("lat")
    depth_here = depths[0]
    weights_qkv = w_qkv[0]
    weights_out = w_out[0]
    level_count, band_rows, strip_cols, model_width = fields.shape
    half_rows = band_rows // 2
    tick_total = MICRO + 3
    block_shape = (WIN_LEV, band_rows, strip_cols, model_width)
    low_valid = (lat_at > 0).astype(jnp.float32)
    high_valid = (lat_at < lat_total - 1).astype(jnp.float32)
    row_valid = jnp.concatenate(
        [
            jnp.ones((half_rows,), jnp.float32) * low_valid,
            jnp.ones((band_rows,), jnp.float32),
            jnp.ones((half_rows,), jnp.float32) * high_valid,
        ]
    )
    mask_field = jnp.broadcast_to(
        row_valid[None, :, None, None], (WIN_LEV, band_rows + 2 * half_rows, strip_cols, 1)
    )
    shifted_valid = to_windows(mask_field, band_rows)[..., 0]
    plain_valid = jnp.ones((strip_cols // WIN_LON, WIN_LEV * band_rows * WIN_LON), jnp.float32)
    actives = [(sublayer < depth_here).astype(jnp.float32) for sublayer in range(MAXL)]
    recv_act = jnp.zeros(block_shape, jnp.bfloat16)
    recv_skip = jnp.zeros(block_shape, jnp.bfloat16)
    outputs = []
    saves_ticks = []
    for tick_no in range(tick_total):
        first_level = WIN_LEV * min(tick_no, MICRO - 1)
        source = fields[first_level : first_level + WIN_LEV].astype(jnp.float32)
        skip_in = recv_skip
        piped_in = recv_act.astype(jnp.float32) + jnp.where(
            segment_at == last_segment, skip_in.astype(jnp.float32), 0.0
        )
        stream = jnp.where(segment_at == 0, source, piped_in)
        layer_saves = []
        for sublayer in range(MAXL):
            stream, kept_state = layer_forward(
                stream,
                sublayer,
                actives[sublayer],
                weights_qkv[sublayer],
                weights_out[sublayer],
                plain_valid,
                shifted_valid,
            )
            layer_saves.append(kept_state)
        out_low = stream.astype(jnp.bfloat16)
        outputs.append(out_low)
        saves_ticks.append(layer_saves)
        if tick_no + 1 < tick_total:
            carried = jnp.where(segment_at == 0, out_low, recv_skip)
            recv_act, recv_skip = passed_along((out_low, carried), "segment", 1)
    stacked = jax.tree.map(stack_all, *saves_ticks)
    grad_back = jnp.zeros(block_shape, jnp.float32)
    recv_gskip = jnp.zeros(block_shape, jnp.float32)
    grads_list = []
    qkv_left = [[] for sublayer in range(MAXL)]
    qkv_right = [[] for sublayer in range(MAXL)]
    out_left = [[] for sublayer in range(MAXL)]
    out_right = [[] for sublayer in range(MAXL)]
    for tick_no in range(tick_total):
        chosen = jnp.clip(tick_no - last_segment + 2 * segment_at, 0, tick_total - 1)
        picked = jax.tree.map(
            partial(lax.dynamic_index_in_dim, index=chosen, axis=0, keepdims=False), stacked
        )
        first_level = WIN_LEV * min(tick_no, MICRO - 1)
        target = cotangent[first_level : first_level + WIN_LEV].astype(jnp.float32) * (
            1.0 if tick_no < MICRO else 0.0
        )
        skip_in = recv_gskip
        from_next = grad_back + jnp.where(segment_at == 0, skip_in, 0.0)
        gradient = jnp.where(segment_at == last_segment, target, from_next)
        for sublayer in reversed(range(MAXL)):
            gradient, qkv_rows, out_rows = layer_backward(
                gradient,
                picked[sublayer],
                sublayer,
                actives[sublayer],
                weights_qkv[sublayer],
                weights_out[sublayer],
            )
            qkv_left[sublayer].append(qkv_rows[0])
            qkv_right[sublayer].append(qkv_rows[1])
            out_left[sublayer].append(out_rows[0])
            out_right[sublayer].append(out_rows[1])
        grads_list.append(gradient)
        if tick_no + 1 < tick_total:
            carried = jnp.where(segment_at == last_segment, gradient, recv_gskip)
            grad_back, recv_gskip = (
                passed_along(for_sending(gradient), "segment", -1).astype(gradient.dtype),
                passed_along(for_sending(carried), "segment", -1).astype(carried.dtype),
            )
    out_stack = jnp.stack(outputs)
    segment_out = jnp.concatenate(
        [
            lax.dynamic_index_in_dim(out_stack, member + segment_at, 0, keepdims=False)
            for member in range(MICRO)
        ],
        axis=0,
    )[None]
    grad_stack = jnp.stack(grads_list)
    segment_grad = jnp.concatenate(
        [
            lax.dynamic_index_in_dim(
                grad_stack, member + last_segment - segment_at, 0, keepdims=False
            )
            for member in range(MICRO)
        ],
        axis=0,
    )[None]
    pieces = []
    for sublayer in range(MAXL):
        pieces.append(
            transpose_dot(
                jnp.concatenate(qkv_left[sublayer], axis=0),
                jnp.concatenate(qkv_right[sublayer], axis=0),
            )
        )
        pieces.append(
            transpose_dot(
                jnp.concatenate(out_left[sublayer], axis=0),
                jnp.concatenate(out_right[sublayer], axis=0),
            )
        )
    grad_term = jnp.concatenate(pieces, axis=1)
    summed = lax.psum_scatter(
        lax.slice_in_dim(
            grad_term,
            0,
            lax.axis_size(("lat", "lon"))
            * (model_width // (lax.axis_size("lat") * lax.axis_size("lon"))),
            axis=0,
        ),
        ("lat", "lon"),
        scatter_dimension=0,
        tiled=True,
    )
    shaped = summed.reshape(summed.shape[0], MAXL, 4 * model_width).transpose(1, 0, 2)
    return (
        segment_out,
        segment_grad,
        shaped[None, :, :, : 3 * model_width],
        shaped[None, :, :, 3 * model_width :],
    )


def solution(mesh):
    placed = (
        P(None, "lat", "lon", None),
        P(None, "lat", "lon", None),
        P("segment"),
        P("segment", None, None, None),
        P("segment", None, None, None),
    )
    return jax.shard_map(
        local,
        mesh=mesh,
        in_specs=placed,
        out_specs=(
            P("segment", None, "lat", "lon", None),
            P("segment", None, "lat", "lon", None),
            P("segment", None, ("lat", "lon"), None),
            P("segment", None, ("lat", "lon"), None),
        ),
        check_vma=False,
    )
```

profile of v0, /device:TPU:8, one launch (start us, length us, event | category | flops | bytes accessed | tf_op | source)
XLA Modules:
  0.0 1452.5 jit_solution(4779503653795007451)
XLA Ops:
  33.9 6.7 collective-permute-start
  86.2 2.9 bitcast_dynamic-update-slice_fusion.9
  89.2 2.9 convolution_convert_fusion.38
  100.1 4.3 collective-permute-start.2
  153.7 6.7 collective-permute-start.4
  186.9 2.9 convolution_convert_fusion.36
  201.2 2.9 bitcast_dynamic-update-slice_fusion.8
  253.5 6.7 collective-permute-start.8
  286.6 2.9 convolution_convert_fusion.34
  300.7 2.9 bitcast_dynamic-update-slice_fusion.7
  353.0 6.7 collective-permute-start.12
  386.3 2.9 convolution_convert_fusion.32
  400.3 2.9 bitcast_dynamic-update-slice_fusion.6
  452.6 7.0 collective-permute-start.16
  473.4 3.7 constant_dynamic-slice_fusion.13
  491.7 3.0 constant_dynamic-slice_fusion.12
  556.6 2.9 concatenate.346
  574.9 5.7 constant_dynamic-slice_fusion.18
  592.8 3.7 fusion.90
  611.7 3.8 convolution_bitcast_fusion.9
  626.3 7.1 collective-permute-start.18
  676.3 3.6 convolution_convert_fusion.28
  684.0 3.6 convolution_convert_fusion.27
  714.0 2.9 fusion.91
  725.2 3.7 convolution_bitcast_fusion.7
  739.9 7.2 collective-permute-start.22
  766.9 3.0 convolution_convert_fusion.24
  771.0 3.8 convolution_convert_fusion.23
  806.8 3.0 fusion.92
  812.7 2.9 copy.1207
  818.2 3.8 convolution_bitcast_fusion.5
  832.9 7.7 collective-permute-start.26
  860.2 3.1 convolution_convert_fusion.20
  864.3 3.8 convolution_convert_fusion.19
  900.0 3.0 fusion.93
  905.9 2.9 copy.1232
  911.4 3.8 convolution_bitcast_fusion.3
  926.2 7.4 collective-permute-start.30
  953.4 3.0 convolution_convert_fusion.16
  957.4 3.7 convolution_convert_fusion.15
  984.4 2.9 fusion.94
  991.2 3.9 convolution_bitcast_fusion.1
  1003.1 6.8 collective-permute-start.34
  1027.7 3.2 fusion.644
  1033.6 6.1 concatenate.345
  1039.7 3.5 fusion.642
  1043.2 3.6 pad_maximum_fusion
  1065.1 377.2 %reduce-scatter.2.cloned.1.call-done = f32[8,4096]{1,0:T(8,128)} async-done(((f32[512,4096]{1,0:T(8,128)}), f32[8,4096]{1,0:T(8,128)}) %reduce-scatter.2.cloned.1.call-update) | async-done | bytes 131088 | tf_op jit(solution)/shard_map/reduce_scatter | solution.py:358
  (1078 shorter events, 860.2 us)
Async XLA Ops:
  7.2 1435.1 %reduce-scatter.2.cloned.1.call-start = ((), (), s32[]{:S(2)}) async-start(), calls=%async_computation.1 | async-start | bytes 8519680 | tf_op jit(solution)/shard_map/reduce_scatter | solution.py:358
  12.5 948.6 %copy-start = (bf16[512,1536]{1,0:T(8,128)(2,1)}, bf16[512,1536]{1,0:T(8,128)(2,1)S(1)}, u32[]{:S(2)}) copy-start(bf16[512,1536]{1,0:T(8,128)(2,1)S(1)} %get-tuple-element.59) | copy-start | bytes 4718596
  30.9 11.5 copy-start.19
  31.9 10.5 copy-start.43
  32.7 42.2 %collective-permute-start.1 = (bf16[2,6,6,512]{3,2,1,0:T(8,128)(2,1)}, bf16[2,6,6,512]{3,2,1,0:T(8,128)(2,1)}, u32[]{:S(2)}, u32[]{:S(2)}) collective-permute-start(bf16[2,6,6,512]{3,2,1,0:T(8,128)(2,1)} %get-tuple-element.167), channel_id=1, source_target_pairs={{4,0},{8,4},{12,8},{16,12},{20,16},{24,20},{28,24},{32,28},{36,32}... | collective-permute-start | bytes 221192 | tf_op jit(solution)/shard_map/ppermute | solution.py:29
  33.9 41.0 %collective-permute-start = (bf16[2,6,6,512]{3,2,1,0:T(8,128)(2,1)}, bf16[2,6,6,512]{3,2,1,0:T(8,128)(2,1)}, u32[]{:S(2)}, u32[]{:S(2)}) collective-permute-start(bf16[2,6,6,512]{3,2,1,0:T(8,128)(2,1)} %get-tuple-element.166), channel_id=1, source_target_pairs={{0,4},{4,8},{8,12},{12,16},{16,20},{20,24},{24,28},{28,32},{32,36}... | collective-permute-start | bytes 221192 | tf_op jit(solution)/shard_map/ppermute | solution.py:27
  60.7 339.5 %copy-start.170 = (f32[2,144]{1,0:T(2,128)}, f32[2,144]{1,0:T(2,128)S(1)}, u32[]{:S(2)}) copy-start(f32[2,144]{1,0:T(2,128)S(1)} %transpose.402) | copy-start | bytes 3460
  98.2 15.4 %collective-permute-start.3 = (bf16[2,12,6,512]{3,2,1,0:T(8,128)(2,1)}, bf16[2,12,6,512]{3,2,1,0:T(8,128)(2,1)}, u32[]{:S(2)}, u32[]{:S(2)}) collective-permute-start(bf16[2,12,6,512]{3,2,1,0:T(8,128)(2,1)} %get-tuple-element.56), channel_id=1, source_target_pairs={{0,64},{64,128},{128,192},{1,65},{65,129},{129,193},{2,66},{66,130... | collective-permute-start | bytes 442376 | tf_op jit(solution)/shard_map/ppermute | solution.py:39
  100.1 13.5 collective-permute-start.2
  152.4 23.2 %collective-permute-start.5 = (bf16[2,6,6,512]{3,2,1,0:T(8,128)(2,1)}, bf16[2,6,6,512]{3,2,1,0:T(8,128)(2,1)}, u32[]{:S(2)}, u32[]{:S(2)}) collective-permute-start(bf16[2,6,6,512]{3,2,1,0:T(8,128)(2,1)} %get-tuple-element.165), channel_id=1, source_target_pairs={{4,0},{8,4},{12,8},{16,12},{20,16},{24,20},{28,24},{32,28},{36,32}... | collective-permute-start | bytes 221192 | tf_op jit(solution)/shard_map/ppermute | solution.py:29
  153.7 21.9 %collective-permute-start.4 = (bf16[2,6,6,512]{3,2,1,0:T(8,128)(2,1)}, bf16[2,6,6,512]{3,2,1,0:T(8,128)(2,1)}, u32[]{:S(2)}, u32[]{:S(2)}) collective-permute-start(bf16[2,6,6,512]{3,2,1,0:T(8,128)(2,1)} %get-tuple-element.164), channel_id=1, source_target_pairs={{0,4},{4,8},{8,12},{12,16},{16,20},{20,24},{24,28},{28,32},{32,36}... | collective-permute-start | bytes 221192 | tf_op jit(solution)/shard_map/ppermute | solution.py:27
  196.0 17.4 %collective-permute-start.7 = (bf16[2,12,6,512]{3,2,1,0:T(8,128)(2,1)}, bf16[2,12,6,512]{3,2,1,0:T(8,128)(2,1)}, u32[]{:S(2)}, u32[]{:S(2)}) collective-permute-start(bf16[2,12,6,512]{3,2,1,0:T(8,128)(2,1)} %get-tuple-element.54), channel_id=1, source_target_pairs={{0,64},{64,128},{128,192},{1,65},{65,129},{129,193},{2,66},{66,130... | collective-permute-start | bytes 442376 | tf_op jit(solution)/shard_map/ppermute | solution.py:39
  198.3 15.1 %collective-permute-start.6 = (bf16[2,12,6,512]{3,2,1,0:T(8,128)(2,1)}, bf16[2,12,6,512]{3,2,1,0:T(8,128)(2,1)}, u32[]{:S(2)}, u32[]{:S(2)}) collective-permute-start(bf16[2,12,6,512]{3,2,1,0:T(8,128)(2,1)} %get-tuple-element.55), channel_id=1, source_target_pairs={{0,64},{64,128},{128,192},{1,65},{65,129},{129,193},{2,66},{66,130... | collective-permute-start | bytes 442376 | tf_op jit(solution)/shard_map/ppermute | solution.py:39
  252.2 23.1 %collective-permute-start.9 = (bf16[2,6,6,512]{3,2,1,0:T(8,128)(2,1)}, bf16[2,6,6,512]{3,2,1,0:T(8,128)(2,1)}, u32[]{:S(2)}, u32[]{:S(2)}) collective-permute-start(bf16[2,6,6,512]{3,2,1,0:T(8,128)(2,1)} %get-tuple-element.163), channel_id=1, source_target_pairs={{4,0},{8,4},{12,8},{16,12},{20,16},{24,20},{28,24},{32,28},{36,32}... | collective-permute-start | bytes 221192 | tf_op jit(solution)/shard_map/ppermute | solution.py:29
  253.5 21.9 %collective-permute-start.8 = (bf16[2,6,6,512]{3,2,1,0:T(8,128)(2,1)}, bf16[2,6,6,512]{3,2,1,0:T(8,128)(2,1)}, u32[]{:S(2)}, u32[]{:S(2)}) collective-permute-start(bf16[2,6,6,512]{3,2,1,0:T(8,128)(2,1)} %get-tuple-element.162), channel_id=1, source_target_pairs={{0,4},{4,8},{8,12},{12,16},{16,20},{20,24},{24,28},{28,32},{32,36}... | collective-permute-start | bytes 221192 | tf_op jit(solution)/shard_map/ppermute | solution.py:27
  295.7 17.2 %collective-permute-start.11 = (bf16[2,12,6,512]{3,2,1,0:T(8,128)(2,1)}, bf16[2,12,6,512]{3,2,1,0:T(8,128)(2,1)}, u32[]{:S(2)}, u32[]{:S(2)}) collective-permute-start(bf16[2,12,6,512]{3,2,1,0:T(8,128)(2,1)} %get-tuple-element.52), channel_id=1, source_target_pairs={{0,64},{64,128},{128,192},{1,65},{65,129},{129,193},{2,66},{66,130... | collective-permute-start | bytes 442376 | tf_op jit(solution)/shard_map/ppermute | solution.py:39
  298.1 14.9 %collective-permute-start.10 = (bf16[2,12,6,512]{3,2,1,0:T(8,128)(2,1)}, bf16[2,12,6,512]{3,2,1,0:T(8,128)(2,1)}, u32[]{:S(2)}, u32[]{:S(2)}) collective-permute-start(bf16[2,12,6,512]{3,2,1,0:T(8,128)(2,1)} %get-tuple-element.53), channel_id=1, source_target_pairs={{0,64},{64,128},{128,192},{1,65},{65,129},{129,193},{2,66},{66,130... | collective-permute-start | bytes 442376 | tf_op jit(solution)/shard_map/ppermute | solution.py:39
  351.8 23.2 %collective-permute-start.13 = (bf16[2,6,6,512]{3,2,1,0:T(8,128)(2,1)}, bf16[2,6,6,512]{3,2,1,0:T(8,128)(2,1)}, u32[]{:S(2)}, u32[]{:S(2)}) collective-permute-start(bf16[2,6,6,512]{3,2,1,0:T(8,128)(2,1)} %get-tuple-element.161), channel_id=1, source_target_pairs={{4,0},{8,4},{12,8},{16,12},{20,16},{24,20},{28,24},{32,28},{36,32}... | collective-permute-start | bytes 221192 | tf_op jit(solution)/shard_map/ppermute | solution.py:29
  353.0 21.9 %collective-permute-start.12 = (bf16[2,6,6,512]{3,2,1,0:T(8,128)(2,1)}, bf16[2,6,6,512]{3,2,1,0:T(8,128)(2,1)}, u32[]{:S(2)}, u32[]{:S(2)}) collective-permute-start(bf16[2,6,6,512]{3,2,1,0:T(8,128)(2,1)} %get-tuple-element.160), channel_id=1, source_target_pairs={{0,4},{4,8},{8,12},{12,16},{16,20},{20,24},{24,28},{28,32},{32,36}... | collective-permute-start | bytes 221192 | tf_op jit(solution)/shard_map/ppermute | solution.py:27
  395.4 17.2 %collective-permute-start.15 = (bf16[2,12,6,512]{3,2,1,0:T(8,128)(2,1)}, bf16[2,12,6,512]{3,2,1,0:T(8,128)(2,1)}, u32[]{:S(2)}, u32[]{:S(2)}) collective-permute-start(bf16[2,12,6,512]{3,2,1,0:T(8,128)(2,1)} %get-tuple-element.50), channel_id=1, source_target_pairs={{0,64},{64,128},{128,192},{1,65},{65,129},{129,193},{2,66},{66,130... | collective-permute-start | bytes 442376 | tf_op jit(solution)/shard_map/ppermute | solution.py:39
  397.9 14.6 %collective-permute-start.14 = (bf16[2,12,6,512]{3,2,1,0:T(8,128)(2,1)}, bf16[2,12,6,512]{3,2,1,0:T(8,128)(2,1)}, u32[]{:S(2)}, u32[]{:S(2)}) collective-permute-start(bf16[2,12,6,512]{3,2,1,0:T(8,128)(2,1)} %get-tuple-element.51), channel_id=1, source_target_pairs={{0,64},{64,128},{128,192},{1,65},{65,129},{129,193},{2,66},{66,130... | collective-permute-start | bytes 442376 | tf_op jit(solution)/shard_map/ppermute | solution.py:39
  451.3 109.8 %collective-permute-start.17 = (bf16[2,6,6,512]{3,2,1,0:T(8,128)(2,1)}, bf16[2,6,6,512]{3,2,1,0:T(8,128)(2,1)}, u32[]{:S(2)}, u32[]{:S(2)}) collective-permute-start(bf16[2,6,6,512]{3,2,1,0:T(8,128)(2,1)} %get-tuple-element.159), channel_id=1, source_target_pairs={{4,0},{8,4},{12,8},{16,12},{20,16},{24,20},{28,24},{32,28},{36,32}... | collective-permute-start | bytes 221192 | tf_op jit(solution)/shard_map/ppermute | solution.py:29
  452.6 108.5 %collective-permute-start.16 = (bf16[2,6,6,512]{3,2,1,0:T(8,128)(2,1)}, bf16[2,6,6,512]{3,2,1,0:T(8,128)(2,1)}, u32[]{:S(2)}, u32[]{:S(2)}) collective-permute-start(bf16[2,6,6,512]{3,2,1,0:T(8,128)(2,1)} %get-tuple-element.158), channel_id=1, source_target_pairs={{0,4},{4,8},{8,12},{12,16},{16,20},{20,24},{24,28},{28,32},{32,36}... | collective-permute-start | bytes 221192 | tf_op jit(solution)/shard_map/ppermute | solution.py:27
  539.6 9.8 copy-start.115
  625.0 36.1 %collective-permute-start.19 = (bf16[2,6,6,1024]{3,0,2,1:T(2,128)(2,1)}, bf16[2,6,6,1024]{3,0,2,1:T(2,128)(2,1)}, u32[]{:S(2)}, u32[]{:S(2)}) collective-permute-start(bf16[2,6,6,1024]{3,0,2,1:T(2,128)(2,1)} %get-tuple-element.133), channel_id=1, source_target_pairs={{4,0},{8,4},{12,8},{16,12},{20,16},{24,20},{28,24},{32,28},{36,32}... | collective-permute-start | bytes 442376 | tf_op jit(solution)/shard_map/ppermute | solution.py:29
  626.3 34.9 %collective-permute-start.18 = (bf16[2,6,6,1024]{3,0,2,1:T(2,128)(2,1)}, bf16[2,6,6,1024]{3,0,2,1:T(2,128)(2,1)}, u32[]{:S(2)}, u32[]{:S(2)}) collective-permute-start(bf16[2,6,6,1024]{3,0,2,1:T(2,128)(2,1)} %get-tuple-element.132), channel_id=1, source_target_pairs={{0,4},{4,8},{8,12},{12,16},{16,20},{20,24},{24,28},{28,32},{32,36}... | collective-permute-start | bytes 442376 | tf_op jit(solution)/shard_map/ppermute | solution.py:27
  697.0 9.4 collective-permute-start.21
  698.4 8.0 collective-permute-start.20
  737.2 10.0 copy-start.81
  737.7 10.6 copy-start.73
  738.6 12.0 collective-permute-start.23
  739.9 12.9 collective-permute-start.22
  789.7 9.4 collective-permute-start.25
  791.0 8.1 collective-permute-start.24
  830.2 10.5 copy-start.83
  830.7 11.1 copy-start.75
  831.6 12.5 collective-permute-start.27
  832.9 13.1 collective-permute-start.26
  883.1 9.2 collective-permute-start.29
  884.4 7.9 collective-permute-start.28
  923.4 10.2 copy-start.85
  923.9 10.8 copy-start.77
  924.9 12.2 collective-permute-start.31
  926.2 13.1 collective-permute-start.30
  970.6 7.5 collective-permute-start.33
  972.1 6.1 collective-permute-start.32
  1001.8 11.2 collective-permute-start.35
  1003.1 9.9 collective-permute-start.34
  (169 other events, 465.8 us)
Sparse Core Ops, SparseCore 0:
  1047.0 395.2 reduce-scatter.1
where the time goes:
time: 1480 us; the launch traced here: 1450 us
  local copies, waits for them, and re-layouts  535 us (36%)
  waiting for transfers between devices  384 us (26%)
  matrix products  270 us (18%)
  other arithmetic  130 us (9%)
  starting transfers between devices  116 us (8%)
  between operations  18.1 us (1%)
    reduce_scatter x1, waiting for transfers between devices, local(): lax.psum_scatter(lax.slice_in_dim(grad_term, 0, lax.axis_size(('lat', 'lo...  377 us
    unnamed x444, local copies, waits for them, and re-layouts  92.3 us
    another operation x48, local copies, waits for them, and re-layouts, stack_all(): return jnp.stack(pieces)  79.2 us
    dynamic_slice x36, local copies, waits for them, and re-layouts, local(): jax.tree.map(partial(lax.dynamic_index_in_dim, index=chosen, axis=0, keep...  78.4 us
    ppermute x10, starting transfers between devices, padded_2(): lax.ppermute(tail, axis, [(i, (i + 1) % count) for i in range(ends)])  70 us
    another operation x31, local copies, waits for them, and re-layouts  46.6 us
    dot_general x30, matrix products, project_back(): lax.dot_general(flattened, weight, (((1,), (1,)), ((), ())), preferred_el...  43.3 us
    dot_general x10, matrix products, attend_back(): jnp.einsum('bhqk,bqhe->bkhe', grad_scores, qheads, preferred_element_type...  36.7 us
  transfers between devices with their start and end apart: 37, of which 4 were waited for; matrix products, arithmetic and copies ran while one was open for 21% of the time, Pallas kernels for 0%

commit v1 on v0

v1 whole, which is shorter than its diff:
```python
from functools import partial

import jax
import jax.numpy as jnp
from jax import lax
from jax.experimental import pallas as pl
from jax.experimental.pallas import tpu as pltpu
from jax.sharding import PartitionSpec as P

HEADS = 8
HS = 64
WIN_LEV = 2
WIN_LON = 6
MAXL = 2
D = 512
PAIRS = 4
HALF = 72
TOK = 144
EPSILON = 1e-05
MESH = pl.DeviceIdType.MESH
F32 = jnp.float32
BF16 = jnp.bfloat16


def dot(a, b, contract):
    return lax.dot_general(a, b, ((contract[:1], contract[1:]), ((), ())), preferred_element_type=F32)


def normalize(stream):
    center = stream - jnp.mean(stream, axis=-1, keepdims=True)
    inverse = lax.rsqrt(jnp.mean(center * center, axis=-1, keepdims=True) + EPSILON)
    return (center * inverse, inverse)


def norm_back(scaled, inverse, gradient):
    middle = gradient - jnp.mean(gradient, axis=-1, keepdims=True)
    return inverse * (middle - scaled * jnp.mean(gradient * scaled, axis=-1, keepdims=True))


def split_heads(value):
    low = lax.broadcasted_iota(jnp.int32, value.shape, 1) < HS
    return jnp.concatenate([jnp.where(low, value, 0.0), jnp.where(low, 0.0, value)], axis=0).astype(BF16)


def join_heads(value):
    count = value.shape[0] // 2
    low = lax.broadcasted_iota(jnp.int32, (count, value.shape[1]), 1) < HS
    return jnp.where(low, value[:count], value[count:])


def window_forward(q2, k, v, valid):
    exponent = jnp.exp(dot(q2, k, (1, 1)) * (HS ** -0.5))
    if valid is not None:
        exponent = exponent * valid
    probs = exponent * (1.0 / jnp.sum(exponent, axis=-1, keepdims=True))
    return probs, join_heads(dot(probs.astype(BF16), v, (1, 0)))


def window_backward(gm2, q2, k, v, probs):
    grad_probs = dot(gm2, v, (1, 1))
    inner = jnp.sum(probs * grad_probs, axis=-1, keepdims=True)
    grad_scores = (probs * (grad_probs - inner) * (HS ** -0.5)).astype(BF16)
    gq = join_heads(dot(grad_scores, k, (1, 0)))
    gk = dot(grad_scores, q2, (0, 0))
    gv = dot(probs.astype(BF16), gm2, (0, 0))
    return gq, gk, gv


def body(
    lat_total,
    fields_ref, cot_ref, active_ref, wqkv_hbm, wout_hbm,
    out_ref, grad_ref, term_ref,
    wqkv_s, wout_s, act_s, xin, gin, stream_s, g_s, outs, out_in, grads, grad_in, handoff,
    nrm, halo, rim, rim_in, xs, invs, probs_s, q2_s, kv_s, left, left_in, right, right_in,
    own_sem, w_send, w_recv, a_sem, x_send, x_recv, g_send, g_recv, o_send, o_recv, s_send, s_recv,
    h_send, h_recv, r_send, r_recv, l_send, l_recv, t_send, t_recv,
):
    seg = lax.axis_index("segment")
    lat = lax.axis_index("lat")
    lon = lax.axis_index("lon")
    core = lax.rem(seg, 2)
    first = seg < 2
    has_prev = lat > 0
    has_next = lat < lat_total - 1
    partner = {"segment": seg + 1 - 2 * core, "lat": lat, "lon": lon}
    across = {"segment": lax.rem(seg + 2, 4), "lat": lat, "lon": lon}
    prev = {"segment": seg, "lat": lax.rem(lat + lat_total - 1, lat_total), "lon": lon}
    nxt = {"segment": seg, "lat": lax.rem(lat + 1, lat_total), "lon": lon}

    def remote(src, dst, send, recv, to):
        return pltpu.make_async_remote_copy(
            src_ref=src, dst_ref=dst, send_sem=send, recv_sem=recv, device_id=to, device_id_type=MESH
        )

    barrier = pltpu.get_barrier_semaphore()
    pl.semaphore_signal(barrier, inc=1, device_id=partner, device_id_type=MESH)
    pl.semaphore_signal(barrier, inc=1, device_id=across, device_id_type=MESH)

    @pl.when(has_prev)
    def _():
        pl.semaphore_signal(barrier, inc=1, device_id=prev, device_id_type=MESH)

    @pl.when(has_next)
    def _():
        pl.semaphore_signal(barrier, inc=1, device_id=nxt, device_id_type=MESH)

    def own_w(layer):
        return (
            pltpu.make_async_copy(wqkv_hbm.at[layer], wqkv_s.at[core, layer], own_sem.at[layer, 0]),
            pltpu.make_async_copy(wout_hbm.at[layer], wout_s.at[core, layer], own_sem.at[layer, 1]),
        )

    def sent_w(layer):
        return (
            remote(wqkv_hbm.at[layer], wqkv_s.at[core, layer], w_send.at[layer, 0], w_recv.at[layer, 0], partner),
            remote(wout_hbm.at[layer], wout_s.at[core, layer], w_send.at[layer, 1], w_recv.at[layer, 1], partner),
        )

    def came_w(layer):
        other = 1 - core
        return (
            remote(wqkv_hbm.at[layer], wqkv_s.at[other, layer], w_send.at[layer, 0], w_recv.at[layer, 0], partner),
            remote(wout_hbm.at[layer], wout_s.at[other, layer], w_send.at[layer, 1], w_recv.at[layer, 1], partner),
        )

    for layer in range(MAXL):
        for copy in own_w(layer):
            copy.start()

    act_s[core] = active_ref[...]

    @pl.when(first)
    def _():
        xin[0] = fields_ref[...]
        xin[1] = jnp.zeros((TOK, D), BF16)

    @pl.when(jnp.logical_not(first))
    def _():
        gin[0] = cot_ref[...]
        gin[1] = jnp.zeros((TOK, D), BF16)

    @pl.when(jnp.logical_not(has_prev))
    def _():
        halo[0, 0] = jnp.zeros((HALF, D), BF16)
        halo[1, 0] = jnp.zeros((HALF, D), BF16)
        rim_in[0, 0] = jnp.zeros((HALF, 2 * D), BF16)
        rim_in[1, 0] = jnp.zeros((HALF, 2 * D), BF16)

    @pl.when(jnp.logical_not(has_next))
    def _():
        halo[0, 1] = jnp.zeros((HALF, D), BF16)
        halo[1, 1] = jnp.zeros((HALF, D), BF16)
        rim_in[0, 1] = jnp.zeros((HALF, 2 * D), BF16)
        rim_in[1, 1] = jnp.zeros((HALF, 2 * D), BF16)

    pl.semaphore_wait(barrier, 2 + has_prev.astype(jnp.int32) + has_next.astype(jnp.int32))

    sent_act = remote(active_ref, act_s.at[core], a_sem.at[0], a_sem.at[1], partner)
    came_act = remote(active_ref, act_s.at[1 - core], a_sem.at[0], a_sem.at[1], partner)
    sent_act.start()
    for layer in range(MAXL):
        for copy in sent_w(layer):
            copy.start()

    def halo_prev(sl):
        return remote(nrm.at[sl, 0], halo.at[sl, 1], h_send.at[sl, 0], h_recv.at[sl, 1], prev)

    def halo_next(sl):
        return remote(nrm.at[sl, 1], halo.at[sl, 0], h_send.at[sl, 1], h_recv.at[sl, 0], nxt)

    def rim_prev(sl):
        return remote(rim.at[sl, 0], rim_in.at[sl, 1], r_send.at[sl, 0], r_recv.at[sl, 1], prev)

    def rim_next(sl):
        return remote(rim.at[sl, 1], rim_in.at[sl, 0], r_send.at[sl, 1], r_recv.at[sl, 0], nxt)

    def start_pair(to_prev, to_next):
        @pl.when(has_prev)
        def _():
            to_prev.start()

        @pl.when(has_next)
        def _():
            to_next.start()

    def arrive_pair(to_prev, to_next):
        @pl.when(has_prev)
        def _():
            to_next.wait_recv()

        @pl.when(has_next)
        def _():
            to_prev.wait_recv()

    def left_pair(to_prev, to_next):
        @pl.when(has_prev)
        def _():
            to_prev.wait_send()

        @pl.when(has_next)
        def _():
            to_next.wait_send()

    def rows_left(sl, layer):
        return remote(left.at[sl, layer], left_in.at[layer], l_send.at[layer], l_recv.at[layer], partner)

    def rows_right(sl, layer):
        return remote(right.at[sl, layer], right_in.at[layer], t_send.at[layer], t_recv.at[layer], partner)

    act_copy = remote(outs.at[1], xin.at[0], x_send.at[0], x_recv.at[0], across)
    skip_copy = remote(outs.at[0], xin.at[1], x_send.at[1], x_recv.at[1], across)
    gact_copy = remote(handoff.at[0], gin.at[0], g_send.at[0], g_recv.at[0], across)
    gskip_copy = remote(handoff.at[1], gin.at[1], g_send.at[1], g_recv.at[1], across)

    def out_copy(sl):
        return remote(outs.at[sl], out_in, o_send, o_recv, partner)

    def grad_copy(sl):
        return remote(grads.at[sl], grad_in, s_send, s_recv, partner)

    prev_valid = has_prev.astype(F32)
    next_valid = has_next.astype(F32)
    key_at = lax.broadcasted_iota(jnp.int32, (1, TOK), 1)
    valid_a = jnp.where(key_at < HALF, prev_valid, 1.0)
    valid_b = jnp.where(key_at < HALF, 1.0, next_valid)

    def weights_ready(sl, layer):
        @pl.when(core == sl)
        def _():
            for copy in own_w(layer):
                copy.wait()

        @pl.when(core != sl)
        def _():
            for copy in came_w(layer):
                copy.wait_recv()

    @pl.when(jnp.logical_not(first))
    def _():
        act_copy.wait_recv()

    stream_s[...] = xin[0].astype(F32)

    def forward(sl, carry):
        stream = stream_s[...]
        scaled, inverse = normalize(stream)
        normed = scaled.astype(BF16)
        xs[sl, 0] = scaled
        invs[sl, 0] = jnp.broadcast_to(inverse, (TOK, 128))
        left[sl, 0, :, :D] = normed
        weights_ready(sl, 0)
        qkv = dot(normed, wqkv_s[sl, 0], (1, 0))
        kv_low = qkv[:, D:].astype(BF16)
        kv_s[sl, 0] = kv_low
        mixed = []
        for p in range(PAIRS):
            at = slice(128 * p, 128 * p + 128)
            q2 = split_heads(qkv[:, at])
            q2_s[sl, 0, p] = q2
            probs, mix = window_forward(q2, kv_low[:, at], kv_low[:, D + 128 * p : D + 128 * p + 128], None)
            probs_s[sl, 0, p] = probs
            mixed.append(mix)
        mixed_low = jnp.concatenate(mixed, axis=1).astype(BF16)
        left[sl, 0, :, D:] = mixed_low
        stream = stream + dot(mixed_low, wout_s[sl, 0], (1, 0))

        scaled, inverse = normalize(stream)
        normed = scaled.astype(BF16)
        nrm[sl, 0] = scaled[:HALF].astype(BF16)
        nrm[sl, 1] = scaled[HALF:].astype(BF16)
        to_prev, to_next = halo_prev(sl), halo_next(sl)
        start_pair(to_prev, to_next)
        xs[sl, 1] = scaled
        invs[sl, 1] = jnp.broadcast_to(inverse, (TOK, 128))
        left[sl, 1, :, :D] = normed
        weights_ready(sl, 1)

        @pl.when(core != sl)
        def _():
            rows_left(sl, 0).start()

        qkv = dot(normed, wqkv_s[sl, 1], (1, 0))
        arrive_pair(to_prev, to_next)
        beside = jnp.concatenate([halo[sl, 0].astype(F32), halo[sl, 1].astype(F32)], axis=0).astype(BF16)
        kv_beside = dot(beside, wqkv_s[sl, 1, :, D:], (1, 0))
        kv_a = jnp.concatenate([kv_beside[:HALF], qkv[:HALF, D:]], axis=0).astype(BF16)
        kv_b = jnp.concatenate([qkv[HALF:, D:], kv_beside[HALF:]], axis=0).astype(BF16)
        kv_s[sl, 1] = kv_a
        kv_s[sl, 2] = kv_b
        mixed = []
        for p in range(PAIRS):
            at = slice(128 * p, 128 * p + 128)
            vat = slice(D + 128 * p, D + 128 * p + 128)
            qa = split_heads(qkv[:HALF, at])
            qb = split_heads(qkv[HALF:, at])
            q2_s[sl, 1, p, :TOK] = qa
            q2_s[sl, 1, p, TOK:] = qb
            probs_a, mix_a = window_forward(qa, kv_a[:, at], kv_a[:, vat], valid_a)
            probs_b, mix_b = window_forward(qb, kv_b[:, at], kv_b[:, vat], valid_b)
            probs_s[sl, 1, p, :TOK] = probs_a
            probs_s[sl, 1, p, TOK:] = probs_b
            mixed.append(jnp.concatenate([mix_a, mix_b], axis=0))
        mixed_low = jnp.concatenate(mixed, axis=1).astype(BF16)
        left[sl, 1, :, D:] = mixed_low

        @pl.when(core != sl)
        def _():
            came_act.wait_recv()
            rows_left(sl, 1).start()

        stream = stream + act_s[sl][0:1, 0:1] * dot(mixed_low, wout_s[sl, 1], (1, 0))
        low = stream.astype(BF16)
        outs[sl] = low

        @pl.when(core != sl)
        def _():
            out_copy(sl).start()

        @pl.when(sl == 0)
        def _():
            @pl.when(first)
            def _():
                skip_copy.start()

            @pl.when(jnp.logical_not(first))
            def _():
                skip_copy.wait_recv()

            stream_s[...] = low.astype(F32) + xin[1].astype(F32)

        return carry

    lax.fori_loop(0, 2, forward, 0)

    @pl.when(first)
    def _():
        act_copy.start()
        gact_copy.wait_recv()

    g_s[...] = gin[0].astype(F32)

    def backward(step, carry):
        sl = 1 - step
        g = g_s[...]
        glow = (g * act_s[sl][0:1, 0:1]).astype(BF16)
        right[sl, 1, :, 3 * D :] = glow
        gm = dot(glow, wout_s[sl, 1], (1, 1))
        gq, gka, gva, gkb, gvb = [], [], [], [], []
        for p in range(PAIRS):
            at = slice(128 * p, 128 * p + 128)
            vat = slice(D + 128 * p, D + 128 * p + 128)
            qa, ka, va = window_backward(
                split_heads(gm[:HALF, at]), q2_s[sl, 1, p, :TOK], kv_s[sl, 1, :, at], kv_s[sl, 1, :, vat],
                probs_s[sl, 1, p, :TOK],
            )
            qb, kb, vb = window_backward(
                split_heads(gm[HALF:, at]), q2_s[sl, 1, p, TOK:], kv_s[sl, 2, :, at], kv_s[sl, 2, :, vat],
                probs_s[sl, 1, p, TOK:],
            )
            gq.append(jnp.concatenate([qa, qb], axis=0))
            gka.append(ka)
            gva.append(va)
            gkb.append(kb)
            gvb.append(vb)
        pair_a = jnp.concatenate(gka + gva, axis=1)
        pair_b = jnp.concatenate(gkb + gvb, axis=1)
        rim[sl, 0] = pair_a[:HALF].astype(BF16)
        rim[sl, 1] = pair_b[HALF:].astype(BF16)
        to_prev, to_next = rim_prev(sl), rim_next(sl)
        start_pair(to_prev, to_next)
        query_low = jnp.concatenate(gq, axis=1).astype(BF16)
        right[sl, 1, :, :D] = query_low
        part = dot(query_low, wqkv_s[sl, 1, :, :D], (1, 1))
        arrive_pair(to_prev, to_next)
        pairs_low = jnp.concatenate(
            [pair_a[HALF:] + rim_in[sl, 0].astype(F32), pair_b[:HALF] + rim_in[sl, 1].astype(F32)], axis=0
        ).astype(BF16)
        right[sl, 1, :, D : 3 * D] = pairs_low

        @pl.when(core != sl)
        def _():
            rows_right(sl, 1).start()

        part = part + dot(pairs_low, wqkv_s[sl, 1, :, D:], (1, 1))
        g = g + norm_back(xs[sl, 1], invs[sl, 1][:, 0:1], part)

        glow = g.astype(BF16)
        right[sl, 0, :, 3 * D :] = glow
        gm = dot(glow, wout_s[sl, 0], (1, 1))
        gq, gk, gv = [], [], []
        for p in range(PAIRS):
            at = slice(128 * p, 128 * p + 128)
            vat = slice(D + 128 * p, D + 128 * p + 128)
            q, k, v = window_backward(
                split_heads(gm[:, at]), q2_s[sl, 0, p], kv_s[sl, 0, :, at], kv_s[sl, 0, :, vat], probs_s[sl, 0, p]
            )
            gq.append(q)
            gk.append(k)
            gv.append(v)
        low = jnp.concatenate(gq + gk + gv, axis=1).astype(BF16)
        right[sl, 0, :, : 3 * D] = low

        @pl.when(core != sl)
        def _():
            rows_right(sl, 0).start()

        part = dot(low, wqkv_s[sl, 0], (1, 1))
        g = g + norm_back(xs[sl, 0], invs[sl, 0][:, 0:1], part)
        grads[sl] = g

        @pl.when(core != sl)
        def _():
            grad_copy(sl).start()

        @pl.when(jnp.logical_not(first))
        def _():
            handoff[1 - step] = g.astype(BF16)

            @pl.when(step == 0)
            def _():
                gskip_copy.start()

            @pl.when(step == 1)
            def _():
                gact_copy.start()

        @pl.when(step == 0)
        def _():
            @pl.when(first)
            def _():
                gskip_copy.wait_recv()

            g_s[...] = g + gin[1].astype(F32)

        return carry

    lax.fori_loop(0, 2, backward, 0)

    def weight_terms(layer, carry):
        rows_left(core, layer).wait_recv()
        rows_right(core, layer).wait_recv()
        for tile in range(4):
            lhs_at = slice(0, D) if tile < 3 else slice(D, 2 * D)
            rhs_at = slice(D * tile, D * tile + D)
            lhs = jnp.concatenate([left[core, layer, :, lhs_at], left_in[layer, :, lhs_at]], axis=0)
            rhs = jnp.concatenate([right[core, layer, :, rhs_at], right_in[layer, :, rhs_at]], axis=0)
            term_ref[layer, tile] = dot(lhs, rhs, (0, 0)).astype(term_ref.dtype)
        return carry

    lax.fori_loop(0, MAXL, weight_terms, 0)

    out_copy(core).wait_recv()
    grad_copy(core).wait_recv()
    out_ref[core] = outs[core]
    out_ref[1 - core] = out_in[...]
    grad_ref[core] = grads[core]
    grad_ref[1 - core] = grad_in[...]

    sent_act.wait_send()

    for layer in range(MAXL):
        for copy in sent_w(layer):
            copy.wait_send()
        rows_left(1 - core, layer).wait_send()
        rows_right(1 - core, layer).wait_send()
    out_copy(1 - core).wait_send()
    grad_copy(1 - core).wait_send()
    for sl in range(2):
        left_pair(halo_prev(sl), halo_next(sl))
        left_pair(rim_prev(sl), rim_next(sl))

    @pl.when(first)
    def _():
        act_copy.wait_send()
        skip_copy.wait_send()

    @pl.when(jnp.logical_not(first))
    def _():
        gact_copy.wait_send()
        gskip_copy.wait_send()


def network(fields, cotangent, active, w_qkv, w_out, lat_total):
    vmem = pl.BlockSpec(memory_space=pltpu.VMEM)
    hbm = pl.BlockSpec(memory_space=pl.ANY)
    dma = pltpu.SemaphoreType.DMA
    scratch = [
        pltpu.VMEM((2, MAXL, D, 3 * D), BF16),
        pltpu.VMEM((2, MAXL, D, D), BF16),
        pltpu.VMEM((2, 8, 128), F32),
        pltpu.VMEM((2, TOK, D), BF16),
        pltpu.VMEM((2, TOK, D), BF16),
        pltpu.VMEM((TOK, D), F32),
        pltpu.VMEM((TOK, D), F32),
        pltpu.VMEM((2, TOK, D), BF16),
        pltpu.VMEM((TOK, D), BF16),
        pltpu.VMEM((2, TOK, D), F32),
        pltpu.VMEM((TOK, D), F32),
        pltpu.VMEM((2, TOK, D), BF16),
        pltpu.VMEM((2, 2, HALF, D), BF16),
        pltpu.VMEM((2, 2, HALF, D), BF16),
        pltpu.VMEM((2, 2, HALF, 2 * D), BF16),
        pltpu.VMEM((2, 2, HALF, 2 * D), BF16),
        pltpu.VMEM((2, MAXL, TOK, D), F32),
        pltpu.VMEM((2, MAXL, TOK, 128), F32),
        pltpu.VMEM((2, MAXL, PAIRS, 2 * TOK, TOK), F32),
        pltpu.VMEM((2, MAXL, PAIRS, 2 * TOK, 128), BF16),
        pltpu.VMEM((2, 3, TOK, 2 * D), BF16),
        pltpu.VMEM((2, MAXL, TOK, 2 * D), BF16),
        pltpu.VMEM((MAXL, TOK, 2 * D), BF16),
        pltpu.VMEM((2, MAXL, TOK, 4 * D), BF16),
        pltpu.VMEM((MAXL, TOK, 4 * D), BF16),
        dma((MAXL, 2)),
        dma((MAXL, 2)),
        dma((MAXL, 2)),
        dma((2,)),
        dma((2,)),
        dma((2,)),
        dma((2,)),
        dma((2,)),
        dma,
        dma,
        dma,
        dma,
        dma((2, 2)),
        dma((2, 2)),
        dma((2, 2)),
        dma((2, 2)),
        dma((MAXL,)),
        dma((MAXL,)),
        dma((MAXL,)),
        dma((MAXL,)),
    ]
    return pl.pallas_call(
        partial(body, lat_total),
        out_shape=(
            jax.ShapeDtypeStruct((2, TOK, D), BF16),
            jax.ShapeDtypeStruct((2, TOK, D), F32),
            jax.ShapeDtypeStruct((MAXL, 4, D, D), BF16),
        ),
        in_specs=[vmem, vmem, vmem, hbm, hbm],
        out_specs=(vmem, vmem, vmem),
        scratch_shapes=scratch,
        compiler_params=pltpu.CompilerParams(
            collective_id=0, has_side_effects=True, vmem_limit_bytes=56 * 1024 * 1024
        ),
        name="network",
    )(fields, cotangent, active, w_qkv, w_out)


def to_rows(cells, core):
    pair = lax.dynamic_slice_in_dim(cells, 2 * core, 2, axis=0)
    return pair.reshape(WIN_LEV, 2, 6, WIN_LON, D).transpose(1, 0, 2, 3, 4).reshape(TOK, D)


def from_rows(rows):
    shaped = rows.reshape(2, 2, WIN_LEV, 6, WIN_LON, D).transpose(0, 2, 1, 3, 4, 5)
    return shaped.reshape(1, 2 * WIN_LEV, 12, WIN_LON, D)


def local(fields, cotangent, depths, w_qkv, w_out):
    core = lax.rem(lax.axis_index("segment"), 2)
    active = jnp.broadcast_to((depths[0] > 1).astype(F32), (8, 128))
    out_rows, grad_rows, terms = network(
        to_rows(fields, core), to_rows(cotangent, core), active, w_qkv[0], w_out[0], lax.axis_size("lat")
    )
    lats, lons = lax.axis_size("lat"), lax.axis_size("lon")
    pieces = terms.reshape(MAXL, 4, lats, lons, D // (lats * lons), D)
    part = lax.all_to_all(pieces, "lon", 3, 3, tiled=True).astype(F32).sum(3).astype(BF16)
    summed = lax.all_to_all(part, "lat", 2, 2, tiled=True).astype(F32).sum(2)
    shaped = summed.transpose(0, 2, 1, 3).reshape(MAXL, -1, 4 * D)
    return (
        from_rows(out_rows),
        from_rows(grad_rows),
        shaped[None, :, :, : 3 * D],
        shaped[None, :, :, 3 * D :],
    )


def solution(mesh):
    placed = (
        P(None, "lat", "lon", None),
        P(None, "lat", "lon", None),
        P("segment"),
        P("segment", None, None, None),
        P("segment", None, None, None),
    )
    return jax.shard_map(
        local,
        mesh=mesh,
        in_specs=placed,
        out_specs=(
            P("segment", None, "lat", "lon", None),
            P("segment", None, "lat", "lon", None),
            P("segment", None, ("lat", "lon"), None),
            P("segment", None, ("lat", "lon"), None),
        ),
        check_vma=False,
    )
```

time: 1480 us -> 213 us (0.14); the launches traced: 1450 us -> 213 us
  local copies, waits for them, and re-layouts: 535 us -> 12.2 us
  waiting for transfers between devices: 384 us -> 23.8 us
  matrix products: 270 us -> 0 us
  other arithmetic: 130 us -> 3.22 us
  Pallas kernels: 0 us -> 106 us
  starting transfers between devices: 116 us -> 18.1 us
  blocking collectives: 0 us -> 48.7 us
  between operations: 18.1 us -> 1.38 us
    reduce_scatter x1 -> x0, waiting for transfers between devices: 377 us -> none  [local(): lax.psum_scatter(lax.slice_in_dim(grad_term, 0, lax.axis_size(('lat', 'lo...]
    dot_general x124 -> x0, matrix products: 242 us -> none  [the longest x30 43.3 us: project_back(): lax.dot_general(flattened, weight, (((1,), (1,)), ((), ())), preferred_el...]
    another operation x89 -> x0, local copies, waits for them, and re-layouts: 140 us -> none  [the longest x48 79.2 us: stack_all(): return jnp.stack(pieces)]
    ppermute x36 -> x0, starting transfers between devices: 116 us -> none  [the longest x10 70 us: padded_2(): lax.ppermute(tail, axis, [(i, (i + 1) % count) for i in range(ends)])]
    pallas_call x0 -> x1, Pallas kernels: none -> 106 us  [network(): pl.pallas_call(partial(body, lat_total), out_shape=(jax.ShapeDtypeStruct(...]
    unnamed x444 -> x4, local copies, waits for them, and re-layouts: 92.3 us -> 0.01 us
    dynamic_slice x40 -> x1, local copies, waits for them, and re-layouts: 80.1 us -> 1.36 us  [to_rows(): pair = lax.dynamic_slice_in_dim(cells, 2 * core, 2, axis=0)]
    convert_element_type x50 -> x0, local copies, waits for them, and re-layouts: 50.4 us -> none  [the longest x15 26.4 us: attend(): mixed_low = mixed.reshape(queried.shape).astype(jnp.bfloat16)]
  transfers between devices with their start and end apart: 37 -> 1, of which waited for: 4 -> 1; matrix products, arithmetic and copies ran while one was open for 21% -> 2% of each run, Pallas kernels for 0% -> 0%
where the time goes in v1:
time: 213 us
  Pallas kernels  106 us (50%)
  blocking collectives  48.7 us (23%)
  waiting for transfers between devices  23.8 us (11%)
  starting transfers between devices  18.1 us (8%)
  local copies, waits for them, and re-layouts  12.2 us (6%)
  other arithmetic  3.22 us (2%)
    pallas_call x1, Pallas kernels, network(): pl.pallas_call(partial(body, lat_total), out_shape=(jax.ShapeDtypeStruct(...  106 us
    all_to_all x1, blocking collectives, local(): lax.all_to_all(pieces, 'lon', 3, 3, tiled=True).astype(F32).sum(3)  48.7 us
    all_to_all x1, waiting for transfers between devices, local(): summed = lax.all_to_all(part, 'lat', 2, 2, tiled=True).astype(F32).sum(2)  23.8 us
    all_to_all x1, starting transfers between devices, local(): summed = lax.all_to_all(part, 'lat', 2, 2, tiled=True).astype(F32).sum(2)  18.1 us
  transfers between devices with their start and end apart: 1, of which 1 were waited for; matrix products, arithmetic and copies ran while one was open for 2% of the time, Pallas kernels for 0%

profile of v1, /device:TPU:8, one launch (start us, length us, event | category | flops | bytes accessed | tf_op | source)
XLA Modules:
  0.0 213.0 jit_solution(3995719169140529429)
XLA Ops:
  1.3 1.4 constant_dynamic-slice_fusion
  2.7 0.7 reshape.43.fields_ref
  3.4 0.7 reshape.45.cot_ref
  4.1 0.6 broadcast_in_dim.9.active_ref
  4.7 105.7 %network.1 = (bf16[2,144,512]{2,1,0:T(8,128)(2,1)}, f32[2,144,512]{2,1,0:T(8,128)}, bf16[2,4,512,512]{3,2,1,0:T(8,128)(2,1)}) custom-call(bf16[144,512]{1,0:T(8,128)(2,1)} %reshape.43.fields_ref, bf16[144,512]{1,0:T(8,128)(2,1)} %reshape.45.cot_ref, f32[8,128]{1,0:T(8,128)} %broadcast_in_dim.9.active_ref, bf16[2,512,1536]{2,1,0:T(8,128)(2,1)} %bitcast.28, ...), custom_call_target="tpu_custom_call" | custom-call | tf_op jit(solution)/shard_map/network/pallas_call | solution.py:534
  110.4 2.7 %copy.34 = bf16[2,4,16,4,8,512]{5,4,2,1,0,3:T(8,128)(2,1)S(1)} copy(bf16[2,4,16,4,8,512]{5,4,3,2,1,0:T(8,128)(2,1)} %bitcast.27) | data formatting | bytes 8388608 | tf_op jit(solution)/shard_map/reshape | solution.py:568
  113.1 48.7 %all_to_all.10 = bf16[2,4,16,4,8,512]{5,4,2,1,0,3:T(8,128)(2,1)} all-to-all(bf16[2,4,16,4,8,512]{5,4,2,1,0,3:T(8,128)(2,1)S(1)} %copy.34), channel_id=1, replica_groups=mesh['segment'=4,'lat'=16,'lon'=4] {'lon'}, dimensions={3} | all-to-all | bytes 8388608 | tf_op jit(solution)/shard_map/all_to_all | solution.py:569
  161.9 0.0 copy-start.1
  161.9 3.1 %reduce_sum.21 = bf16[2,4,16,8,512]{4,3,2,1,0:T(8,128)(2,1)S(1)} reduce(bf16[2,4,16,4,8,512]{5,4,2,1,0,3:T(8,128)(2,1)} %all_to_all.10, bf16[]{:T(256)} %constant.20.clone.1), dimensions={3}, to_apply=%region_0.0 | reduce | flops 1572864 | bytes 5242882 | tf_op jit(solution)/shard_map/reduce_sum | solution.py:569
  164.9 0.0 copy-start
  165.0 1.1 copy.35
  166.1 18.1 %all-to-all-start.1 = ((bf16[2,4,16,8,512]{4,3,1,0,2:T(8,128)(2,1)}), bf16[2,4,16,8,512]{4,3,1,0,2:T(8,128)(2,1)S(1)}, u32[]{:S(2)}, u32[]{:S(2)}) async-start(bf16[2,4,16,8,512]{4,3,1,0,2:T(8,128)(2,1)} %copy.35), calls=%async_computation.1 | async-start | bytes 2097152 | tf_op jit(solution)/shard_map/all_to_all | solution.py:570
  184.2 0.0 copy-done.1
  184.2 0.3 copy.30
  184.5 0.2 copy.31
  184.7 0.8 reshape.47
  185.6 0.0 copy-done
  185.6 0.5 copy.32
  186.0 0.5 copy.33
  186.5 1.3 reshape.49
  187.8 23.8 %all-to-all-done.1 = bf16[2,4,16,8,512]{4,3,1,0,2:T(8,128)(2,1)S(1)} async-done(((bf16[2,4,16,8,512]{4,3,1,0,2:T(8,128)(2,1)}), bf16[2,4,16,8,512]{4,3,1,0,2:T(8,128)(2,1)S(1)}, u32[]{:S(2)}, u32[]{:S(2)}) %all-to-all-start.1) | async-done | bytes 1048608 | tf_op jit(solution)/shard_map/all_to_all | solution.py:570
  211.6 0.1 convert_reduce_fusion
  211.7 0.6 slice_bitcast_fusion.1
  212.3 0.6 slice_bitcast_fusion
  (2 shorter events, 0.0 us)
Async XLA Ops:
  161.9 22.3 %copy-start.1 = (bf16[2,144,512]{2,1,0:T(8,128)(2,1)S(1)}, bf16[2,144,512]{2,1,0:T(8,128)(2,1)}, u32[]{:S(2)}) copy-start(bf16[2,144,512]{2,1,0:T(8,128)(2,1)} %get-tuple-element.7) | copy-start | bytes 884740
  164.9 20.6 %copy-start = (f32[2,144,512]{2,1,0:T(8,128)S(1)}, f32[2,144,512]{2,1,0:T(8,128)}, u32[]{:S(2)}) copy-start(f32[2,144,512]{2,1,0:T(8,128)} %get-tuple-element.8) | copy-start | bytes 1769476
  166.1 45.5 %all-to-all-start.1 = ((bf16[2,4,16,8,512]{4,3,1,0,2:T(8,128)(2,1)}), bf16[2,4,16,8,512]{4,3,1,0,2:T(8,128)(2,1)S(1)}, u32[]{:S(2)}, u32[]{:S(2)}) async-start(bf16[2,4,16,8,512]{4,3,1,0,2:T(8,128)(2,1)} %copy.35), calls=%async_computation.1 | async-start | bytes 2097152 | tf_op jit(solution)/shard_map/all_to_all | solution.py:570

commit v2 on v1

--- a/solution.py
+++ b/solution.py
@@ -67,13 +67,15 @@
 
 
 def body(
-    lat_total,
+    lat_total, lon_total,
     fields_ref, cot_ref, active_ref, wqkv_hbm, wout_hbm,
     out_ref, grad_ref, term_ref,
     wqkv_s, wout_s, act_s, xin, gin, stream_s, g_s, outs, out_in, grads, grad_in, handoff,
     nrm, halo, rim, rim_in, xs, invs, probs_s, q2_s, kv_s, left, left_in, right, right_in,
+    part_s, part_in, mid_s, mid_in, fin_s, fin_in,
     own_sem, w_send, w_recv, a_sem, x_send, x_recv, g_send, g_recv, o_send, o_recv, s_send, s_recv,
     h_send, h_recv, r_send, r_recv, l_send, l_recv, t_send, t_recv,
+    y_send, y_recv, z_send, z_recv, f_send, f_recv,
 ):
     seg = lax.axis_index("segment")
     lat = lax.axis_index("lat")
@@ -96,13 +98,22 @@
     pl.semaphore_signal(barrier, inc=1, device_id=partner, device_id_type=MESH)
     pl.semaphore_signal(barrier, inc=1, device_id=across, device_id_type=MESH)
 
-    @pl.when(has_prev)
-    def _():
-        pl.semaphore_signal(barrier, inc=1, device_id=prev, device_id_type=MESH)
-
-    @pl.when(has_next)
-    def _():
-        pl.semaphore_signal(barrier, inc=1, device_id=nxt, device_id_type=MESH)
+    def lon_peer(hop):
+        return {"segment": seg, "lat": lat, "lon": lax.rem(lon + hop, lon_total)}
+
+    def lat_peer(hop):
+        return {"segment": seg, "lat": lax.rem(lat + hop, lat_total), "lon": lon}
+
+    def greet_lon(hop, carry):
+        pl.semaphore_signal(barrier, inc=1, device_id=lon_peer(hop), device_id_type=MESH)
+        return carry
+
+    def greet_lat(hop, carry):
+        pl.semaphore_signal(barrier, inc=1, device_id=lat_peer(hop), device_id_type=MESH)
+        return carry
+
+    lax.fori_loop(1, lon_total, greet_lon, 0)
+    lax.fori_loop(1, lat_total, greet_lat, 0)
 
     def own_w(layer):
         return (
@@ -153,7 +164,7 @@
         rim_in[0, 1] = jnp.zeros((HALF, 2 * D), BF16)
         rim_in[1, 1] = jnp.zeros((HALF, 2 * D), BF16)
 
-    pl.semaphore_wait(barrier, 2 + has_prev.astype(jnp.int32) + has_next.astype(jnp.int32))
+    pl.semaphore_wait(barrier, lon_total + lat_total)
 
     sent_act = remote(active_ref, act_s.at[core], a_sem.at[0], a_sem.at[1], partner)
     came_act = remote(active_ref, act_s.at[1 - core], a_sem.at[0], a_sem.at[1], partner)
@@ -201,11 +212,61 @@
         def _():
             to_next.wait_send()
 
-    def rows_left(sl, layer):
-        return remote(left.at[sl, layer], left_in.at[layer], l_send.at[layer], l_recv.at[layer], partner)
-
-    def rows_right(sl, layer):
-        return remote(right.at[sl, layer], right_in.at[layer], t_send.at[layer], t_recv.at[layer], partner)
+    def rows_left(unit):
+        return remote(left.at[unit], left_in.at[unit], l_send.at[unit], l_recv.at[unit], partner)
+
+    def rows_right(unit):
+        return remote(right.at[unit, 1 - core], right_in.at[unit], t_send.at[unit], t_recv.at[unit], partner)
+
+    def part_copy(unit, hop):
+        to = lax.rem(lon + hop, lon_total)
+        return remote(
+            part_s.at[unit, to], part_in.at[unit, hop - 1], y_send.at[unit, hop - 1], y_recv.at[unit, hop - 1], lon_peer(hop)
+        )
+
+    def mid_copy(unit, hop):
+        to = lax.rem(lat + hop, lat_total)
+        return remote(
+            mid_s.at[unit, to], mid_in.at[unit, hop - 1], z_send.at[unit, hop - 1], z_recv.at[unit, hop - 1], lat_peer(hop)
+        )
+
+    def fin_copy(layer):
+        return remote(fin_s.at[1 - core, layer], fin_in.at[layer], f_send.at[layer], f_recv.at[layer], partner)
+
+    def weight_term(unit):
+        rows_left(unit).wait_recv()
+        rows_right(unit).wait_recv()
+        normed = jnp.concatenate([left[unit, 0], left_in[unit, 0]], axis=0)
+        second = jnp.concatenate([left[unit, core], left_in[unit, core]], axis=0)
+        grads_low = jnp.concatenate([right[unit, core], right_in[unit]], axis=0)
+        group = lat_total * lon_total
+        one = dot(normed, grads_low[:, :D], (0, 0)).reshape(lat_total, lon_total, D // group, D)
+        two = dot(second, grads_low[:, D:], (0, 0)).reshape(lat_total, lon_total, D // group, D)
+        both = jnp.concatenate([one, two], axis=2).astype(BF16)
+        for to in range(lon_total):
+            part_s[unit, to] = both[:, to]
+        for hop in range(1, lon_total):
+            part_copy(unit, hop).start()
+
+    def middle(unit, carry):
+        total = part_s[unit, lon].astype(F32)
+        for hop in range(1, lon_total):
+            part_copy(unit, hop).wait_recv()
+            total = total + part_in[unit, hop - 1].astype(F32)
+        mid_s[unit] = total.astype(BF16)
+
+        def send(hop, inner):
+            mid_copy(unit, hop).start()
+            return inner
+
+        return lax.fori_loop(1, lat_total, send, carry)
+
+    def last(unit):
+        def add(hop, total):
+            mid_copy(unit, hop).wait_recv()
+            return total + mid_in[unit, hop - 1].astype(F32)
+
+        return lax.fori_loop(1, lat_total, add, mid_s[unit, lat].astype(F32))
 
     act_copy = remote(outs.at[1], xin.at[0], x_send.at[0], x_recv.at[0], across)
     skip_copy = remote(outs.at[0], xin.at[1], x_send.at[1], x_recv.at[1], across)
@@ -247,7 +308,7 @@
         normed = scaled.astype(BF16)
         xs[sl, 0] = scaled
         invs[sl, 0] = jnp.broadcast_to(inverse, (TOK, 128))
-        left[sl, 0, :, :D] = normed
+        left[2 * sl, 0] = normed
         weights_ready(sl, 0)
         qkv = dot(normed, wqkv_s[sl, 0], (1, 0))
         kv_low = qkv[:, D:].astype(BF16)
@@ -261,7 +322,7 @@
             probs_s[sl, 0, p] = probs
             mixed.append(mix)
         mixed_low = jnp.concatenate(mixed, axis=1).astype(BF16)
-        left[sl, 0, :, D:] = mixed_low
+        left[2 * sl, 1] = mixed_low
         stream = stream + dot(mixed_low, wout_s[sl, 0], (1, 0))
 
         scaled, inverse = normalize(stream)
@@ -272,13 +333,10 @@
         start_pair(to_prev, to_next)
         xs[sl, 1] = scaled
         invs[sl, 1] = jnp.broadcast_to(inverse, (TOK, 128))
-        left[sl, 1, :, :D] = normed
+        left[2 * sl + 1, 0] = normed
         weights_ready(sl, 1)
 
-        @pl.when(core != sl)
-        def _():
-            rows_left(sl, 0).start()
-
+        rows_left(2 * sl).start()
         qkv = dot(normed, wqkv_s[sl, 1], (1, 0))
         arrive_pair(to_prev, to_next)
         beside = jnp.concatenate([halo[sl, 0].astype(F32), halo[sl, 1].astype(F32)], axis=0).astype(BF16)
@@ -301,12 +359,13 @@
             probs_s[sl, 1, p, TOK:] = probs_b
             mixed.append(jnp.concatenate([mix_a, mix_b], axis=0))
         mixed_low = jnp.concatenate(mixed, axis=1).astype(BF16)
-        left[sl, 1, :, D:] = mixed_low
+        left[2 * sl + 1, 1] = mixed_low
+
+        rows_left(2 * sl + 1).start()
 
         @pl.when(core != sl)
         def _():
             came_act.wait_recv()
-            rows_left(sl, 1).start()
 
         stream = stream + act_s[sl][0:1, 0:1] * dot(mixed_low, wout_s[sl, 1], (1, 0))
         low = stream.astype(BF16)
@@ -343,7 +402,7 @@
         sl = 1 - step
         g = g_s[...]
         glow = (g * act_s[sl][0:1, 0:1]).astype(BF16)
-        right[sl, 1, :, 3 * D :] = glow
+        right[2 * sl + 1, 1, :, D:] = glow
         gm = dot(glow, wout_s[sl, 1], (1, 1))
         gq, gka, gva, gkb, gvb = [], [], [], [], []
         for p in range(PAIRS):
@@ -369,23 +428,26 @@
         to_prev, to_next = rim_prev(sl), rim_next(sl)
         start_pair(to_prev, to_next)
         query_low = jnp.concatenate(gq, axis=1).astype(BF16)
-        right[sl, 1, :, :D] = query_low
+        right[2 * sl + 1, 0, :, :D] = query_low
         part = dot(query_low, wqkv_s[sl, 1, :, :D], (1, 1))
+
+        @pl.when(step == 1)
+        def _():
+            weight_term(2)
+
         arrive_pair(to_prev, to_next)
         pairs_low = jnp.concatenate(
             [pair_a[HALF:] + rim_in[sl, 0].astype(F32), pair_b[:HALF] + rim_in[sl, 1].astype(F32)], axis=0
         ).astype(BF16)
-        right[sl, 1, :, D : 3 * D] = pairs_low
-
-        @pl.when(core != sl)
-        def _():
-            rows_right(sl, 1).start()
-
+        right[2 * sl + 1, 0, :, D:] = pairs_low[:, :D]
+        right[2 * sl + 1, 1, :, :D] = pairs_low[:, D:]
+
+        rows_right(2 * sl + 1).start()
         part = part + dot(pairs_low, wqkv_s[sl, 1, :, D:], (1, 1))
         g = g + norm_back(xs[sl, 1], invs[sl, 1][:, 0:1], part)
 
         glow = g.astype(BF16)
-        right[sl, 0, :, 3 * D :] = glow
+        right[2 * sl, 1, :, D:] = glow
         gm = dot(glow, wout_s[sl, 0], (1, 1))
         gq, gk, gv = [], [], []
         for p in range(PAIRS):
@@ -398,12 +460,10 @@
             gk.append(k)
             gv.append(v)
         low = jnp.concatenate(gq + gk + gv, axis=1).astype(BF16)
-        right[sl, 0, :, : 3 * D] = low
-
-        @pl.when(core != sl)
-        def _():
-            rows_right(sl, 0).start()
-
+        right[2 * sl, 0] = low[:, : 2 * D]
+        right[2 * sl, 1, :, :D] = low[:, 2 * D :]
+
+        rows_right(2 * sl).start()
         part = dot(low, wqkv_s[sl, 0], (1, 1))
         g = g + norm_back(xs[sl, 0], invs[sl, 0][:, 0:1], part)
         grads[sl] = g
@@ -432,22 +492,30 @@
 
             g_s[...] = g + gin[1].astype(F32)
 
+        weight_term(2 * sl + 1)
         return carry
 
     lax.fori_loop(0, 2, backward, 0)
-
-    def weight_terms(layer, carry):
-        rows_left(core, layer).wait_recv()
-        rows_right(core, layer).wait_recv()
-        for tile in range(4):
-            lhs_at = slice(0, D) if tile < 3 else slice(D, 2 * D)
-            rhs_at = slice(D * tile, D * tile + D)
-            lhs = jnp.concatenate([left[core, layer, :, lhs_at], left_in[layer, :, lhs_at]], axis=0)
-            rhs = jnp.concatenate([right[core, layer, :, rhs_at], right_in[layer, :, rhs_at]], axis=0)
-            term_ref[layer, tile] = dot(lhs, rhs, (0, 0)).astype(term_ref.dtype)
+    weight_term(0)
+
+    lax.fori_loop(0, 4, lambda step, carry: middle(3 - step, carry), 0)
+
+    def finish(step, carry):
+        unit = 3 - step
+        owner, layer = unit // 2, lax.rem(unit, 2)
+        fin_s[owner, layer] = last(unit)
+
+        @pl.when(owner != core)
+        def _():
+            fin_copy(layer).start()
+
         return carry
 
-    lax.fori_loop(0, MAXL, weight_terms, 0)
+    lax.fori_loop(0, 4, finish, 0)
+    for layer in range(MAXL):
+        fin_copy(layer).wait_recv()
+        term_ref[layer, core] = fin_s[core, layer]
+        term_ref[layer, 1 - core] = fin_in[layer]
 
     out_copy(core).wait_recv()
     grad_copy(core).wait_recv()
@@ -461,8 +529,18 @@
     for layer in range(MAXL):
         for copy in sent_w(layer):
             copy.wait_send()
-        rows_left(1 - core, layer).wait_send()
-        rows_right(1 - core, layer).wait_send()
+        fin_copy(layer).wait_send()
+    for unit in range(4):
+        rows_left(unit).wait_send()
+        rows_right(unit).wait_send()
+        for hop in range(1, lon_total):
+            part_copy(unit, hop).wait_send()
+
+        def sent(hop, carry):
+            mid_copy(unit, hop).wait_send()
+            return carry
+
+        lax.fori_loop(1, lat_total, sent, 0)
     out_copy(1 - core).wait_send()
     grad_copy(1 - core).wait_send()
     for sl in range(2):
@@ -480,7 +558,8 @@
         gskip_copy.wait_send()
 
 
-def network(fields, cotangent, active, w_qkv, w_out, lat_total):
+def network(fields, cotangent, active, w_qkv, w_out, lat_total, lon_total):
+    piece = 2 * D // (lat_total * lon_total)
     vmem = pl.BlockSpec(memory_space=pltpu.VMEM)
     hbm = pl.BlockSpec(memory_space=pl.ANY)
     dma = pltpu.SemaphoreType.DMA
@@ -506,10 +585,16 @@
         pltpu.VMEM((2, MAXL, PAIRS, 2 * TOK, TOK), F32),
         pltpu.VMEM((2, MAXL, PAIRS, 2 * TOK, 128), BF16),
         pltpu.VMEM((2, 3, TOK, 2 * D), BF16),
-        pltpu.VMEM((2, MAXL, TOK, 2 * D), BF16),
-        pltpu.VMEM((MAXL, TOK, 2 * D), BF16),
-        pltpu.VMEM((2, MAXL, TOK, 4 * D), BF16),
-        pltpu.VMEM((MAXL, TOK, 4 * D), BF16),
+        pltpu.VMEM((4, 2, TOK, D), BF16),
+        pltpu.VMEM((4, 2, TOK, D), BF16),
+        pltpu.VMEM((4, 2, TOK, 2 * D), BF16),
+        pltpu.VMEM((4, TOK, 2 * D), BF16),
+        pltpu.VMEM((4, lon_total, lat_total, piece, D), BF16),
+        pltpu.VMEM((4, lon_total - 1, lat_total, piece, D), BF16),
+        pltpu.VMEM((4, lat_total, piece, D), BF16),
+        pltpu.VMEM((4, lat_total - 1, piece, D), BF16),
+        pltpu.VMEM((2, MAXL, piece, D), F32),
+        pltpu.VMEM((MAXL, piece, D), F32),
         dma((MAXL, 2)),
         dma((MAXL, 2)),
         dma((MAXL, 2)),
@@ -526,17 +611,23 @@
         dma((2, 2)),
         dma((2, 2)),
         dma((2, 2)),
-        dma((MAXL,)),
-        dma((MAXL,)),
+        dma((4,)),
+        dma((4,)),
+        dma((4,)),
+        dma((4,)),
+        dma((4, lon_total - 1)),
+        dma((4, lon_total - 1)),
+        dma((4, lat_total - 1)),
+        dma((4, lat_total - 1)),
         dma((MAXL,)),
         dma((MAXL,)),
     ]
     return pl.pallas_call(
-        partial(body, lat_total),
+        partial(body, lat_total, lon_total),
         out_shape=(
             jax.ShapeDtypeStruct((2, TOK, D), BF16),
             jax.ShapeDtypeStruct((2, TOK, D), F32),
-            jax.ShapeDtypeStruct((MAXL, 4, D, D), BF16),
+            jax.ShapeDtypeStruct((MAXL, 2, piece, D), F32),
         ),
         in_specs=[vmem, vmem, vmem, hbm, hbm],
         out_specs=(vmem, vmem, vmem),
@@ -562,13 +653,10 @@
     core = lax.rem(lax.axis_index("segment"), 2)
     active = jnp.broadcast_to((depths[0] > 1).astype(F32), (8, 128))
     out_rows, grad_rows, terms = network(
-        to_rows(fields, core), to_rows(cotangent, core), active, w_qkv[0], w_out[0], lax.axis_size("lat")
+        to_rows(fields, core), to_rows(cotangent, core), active, w_qkv[0], w_out[0],
+        lax.axis_size("lat"), lax.axis_size("lon"),
     )
-    lats, lons = lax.axis_size("lat"), lax.axis_size("lon")
-    pieces = terms.reshape(MAXL, 4, lats, lons, D // (lats * lons), D)
-    part = lax.all_to_all(pieces, "lon", 3, 3, tiled=True).astype(F32).sum(3).astype(BF16)
-    summed = lax.all_to_all(part, "lat", 2, 2, tiled=True).astype(F32).sum(2)
-    shaped = summed.transpose(0, 2, 1, 3).reshape(MAXL, -1, 4 * D)
+    shaped = terms.reshape(MAXL, 4, -1, D).transpose(0, 2, 1, 3).reshape(MAXL, -1, 4 * D)
     return (
         from_rows(out_rows),
         from_rows(grad_rows),

time: 213 us -> 172 us (0.81)
  Pallas kernels: 106 us -> 157 us
  blocking collectives: 48.7 us -> 0 us
  waiting for transfers between devices: 23.8 us -> 0 us
  starting transfers between devices: 18.1 us -> 0 us
  other arithmetic: 3.22 us -> 0 us
    pallas_call x1, Pallas kernels: 106 us -> 157 us  [network(): pl.pallas_call(partial(body, lat_total, lon_total), out_shape=(jax.ShapeD...]
    all_to_all x1 -> x0, blocking collectives: 48.7 us -> none  [local(): lax.all_to_all(pieces, 'lon', 3, 3, tiled=True).astype(F32).sum(3)]
    all_to_all x1 -> x0, waiting for transfers between devices: 23.8 us -> none  [local(): summed = lax.all_to_all(part, 'lat', 2, 2, tiled=True).astype(F32).sum(2)]
    all_to_all x1 -> x0, starting transfers between devices: 18.1 us -> none  [local(): summed = lax.all_to_all(part, 'lat', 2, 2, tiled=True).astype(F32).sum(2)]
    reduce_sum x2 -> x0, other arithmetic: 3.22 us -> none  [the longest x1 3.07 us: local(): lax.all_to_all(pieces, 'lon', 3, 3, tiled=True).astype(F32).sum(3)]
    reshape x1 -> x0, local copies, waits for them, and re-layouts: 2.74 us -> none  [local(): pieces = terms.reshape(MAXL, 4, lats, lons, D // (lats * lons), D)]
  transfers between devices with their start and end apart: 1 -> 0, of which waited for: 1 -> 0; matrix products, arithmetic and copies ran while one was open for 2% -> 0% of each run, Pallas kernels for 0% -> 0%
where the time goes in v2:
time: 172 us; the launch traced here: 171 us
  Pallas kernels  157 us (91%)
  local copies, waits for them, and re-layouts  12 us (7%)
    pallas_call x1, Pallas kernels, network(): pl.pallas_call(partial(body, lat_total, lon_total), out_shape=(jax.ShapeD...  157 us

profile of v2, /device:TPU:8, one launch (start us, length us, event | category | flops | bytes accessed | tf_op | source)
XLA Modules:
  0.0 170.7 jit_solution(9255820309174224917)
XLA Ops:
  1.3 0.6 broadcast_in_dim.9.active_ref
  1.9 1.4 constant_dynamic-slice_fusion
  3.3 0.7 reshape.43.fields_ref
  4.0 0.7 reshape.45.cot_ref
  4.7 157.4 %network.1 = (bf16[2,144,512]{2,1,0:T(8,128)(2,1)}, f32[2,144,512]{2,1,0:T(8,128)}, f32[2,2,16,512]{3,2,1,0:T(8,128)}) custom-call(bf16[144,512]{1,0:T(8,128)(2,1)} %reshape.43.fields_ref, bf16[144,512]{1,0:T(8,128)(2,1)} %reshape.45.cot_ref, f32[8,128]{1,0:T(8,128)} %broadcast_in_dim.9.active_ref, bf16[2,512,1536]{2,1,0:T(8,128)(2,1)} %bitcast.28, ...), custom_call_target="tpu_custom_call" | custom-call | tf_op jit(solution)/shard_map/network/pallas_call | solution.py:625
  162.1 1.3 copy.17
  163.4 0.2 copy.18
  163.6 0.8 reshape.47
  164.5 1.4 slice_bitcast_fusion.1
  165.8 1.5 slice_bitcast_fusion
  167.4 1.5 copy.19
  168.9 0.5 copy.20
  169.4 1.3 reshape.49
  (2 shorter events, 0.0 us)

commit v3 on v2

v3 whole, which is shorter than its diff:
```python
from functools import partial

import jax
import jax.numpy as jnp
from jax import lax
from jax.experimental import pallas as pl
from jax.experimental.pallas import tpu as pltpu
from jax.sharding import PartitionSpec as P

HEADS = 8
HS = 64
WIN_LEV = 2
WIN_LON = 6
MAXL = 2
D = 512
PAIRS = 4
HALF = 72
TOK = 144
EPSILON = 1e-05
MESH = pl.DeviceIdType.MESH
F32 = jnp.float32
BF16 = jnp.bfloat16


def dot(a, b, contract):
    return lax.dot_general(a, b, ((contract[:1], contract[1:]), ((), ())), preferred_element_type=F32)


def normalize(stream):
    center = stream - jnp.mean(stream, axis=-1, keepdims=True)
    inverse = lax.rsqrt(jnp.mean(center * center, axis=-1, keepdims=True) + EPSILON)
    return (center * inverse, inverse)


def norm_back(scaled, inverse, gradient):
    middle = gradient - jnp.mean(gradient, axis=-1, keepdims=True)
    return inverse * (middle - scaled * jnp.mean(gradient * scaled, axis=-1, keepdims=True))


def split_heads(value):
    low = lax.broadcasted_iota(jnp.int32, value.shape, 1) < HS
    return jnp.concatenate([jnp.where(low, value, 0.0), jnp.where(low, 0.0, value)], axis=0).astype(BF16)


def join_heads(value):
    count = value.shape[0] // 2
    low = lax.broadcasted_iota(jnp.int32, (count, value.shape[1]), 1) < HS
    return jnp.where(low, value[:count], value[count:])


def window_forward(q2, k, v, valid):
    exponent = jnp.exp(dot(q2, k, (1, 1)) * (HS ** -0.5))
    if valid is not None:
        exponent = exponent * valid
    probs = exponent * (1.0 / jnp.sum(exponent, axis=-1, keepdims=True))
    return probs, join_heads(dot(probs.astype(BF16), v, (1, 0)))


def window_backward(gm2, q2, k, v, probs):
    grad_probs = dot(gm2, v, (1, 1))
    inner = jnp.sum(probs * grad_probs, axis=-1, keepdims=True)
    grad_scores = (probs * (grad_probs - inner) * (HS ** -0.5)).astype(BF16)
    gq = dot(grad_scores, k, (1, 0))
    gk = dot(grad_scores, q2, (0, 0))
    gv = dot(probs.astype(BF16), gm2, (0, 0))
    return gq, gk, gv


def body(
    lat_total, lon_total,
    fields_ref, cot_ref, depth_ref, wqkv_hbm, wout_hbm,
    out_ref, grad_ref, qkv_ref, wo_ref,
    wqkv_s, wout_s, act_s, stage, xin, gin, stream_s, g_s, outs, out_in, grads, grad_in, handoff,
    nrm, halo, rim, rim_in, xs, invs, probs_s, q2_s, kv_s, left, left_in, right, right_in,
    part_s, one_in, one_s, two_in, two_s, three_in, col_s, col_in, fin_s, fin_in,
    own_sem, w_send, w_recv, a_sem, i_sem, x_send, x_recv, g_send, g_recv, o_send, o_recv, s_send, s_recv,
    h_send, h_recv, r_send, r_recv, l_send, l_recv, t_send, t_recv,
    p_send, p_recv, z_send, z_recv, f_send, f_recv,
):
    seg = lax.axis_index("segment")
    lat = lax.axis_index("lat")
    lon = lax.axis_index("lon")
    core = lax.rem(seg, 2)
    first = seg < 2
    high = lax.rem(lat, 2)
    z_at = lat // 2
    z_total = lat_total // 2
    at_home = core == high
    has_far = jnp.where(core == 0, lat > 1, lat < lat_total - 2)
    other = seg + 1 - 2 * core
    partner = {"segment": other, "lat": lat, "lon": lon}
    across = {"segment": lax.rem(seg + 2, 4), "lat": lat, "lon": lon}
    beyond = {"segment": other, "lat": lax.rem(lat + lat_total - 2 + 4 * core, lat_total), "lon": lon}
    twin_lat = lat + 1 - 2 * high
    twin = {"segment": seg, "lat": twin_lat, "lon": lon}
    diagonal = {"segment": other, "lat": twin_lat, "lon": lon}

    def remote(src, dst, send, recv, to):
        return pltpu.make_async_remote_copy(
            src_ref=src, dst_ref=dst, send_sem=send, recv_sem=recv, device_id=to, device_id_type=MESH
        )

    barrier = pltpu.get_barrier_semaphore()
    pl.semaphore_signal(barrier, inc=1, device_id=partner, device_id_type=MESH)
    pl.semaphore_signal(barrier, inc=1, device_id=across, device_id_type=MESH)
    pl.semaphore_signal(barrier, inc=1, device_id=diagonal, device_id_type=MESH)

    @pl.when(has_far)
    def _():
        pl.semaphore_signal(barrier, inc=1, device_id=beyond, device_id_type=MESH)

    side, end = lax.rem((lon + 1) // 2, 2), lon // 2
    lon_side = lon + 1 - 2 * lax.rem(lon, 2)
    lon_end = lon_total - 1 - lon
    flat = core == 0
    peer_one = {"segment": seg, "lat": jnp.where(flat, lat, twin_lat), "lon": jnp.where(flat, lon_side, lon)}
    peer_two = {"segment": seg, "lat": lat, "lon": lon_end}
    peer_three = {"segment": seg, "lat": jnp.where(flat, twin_lat, lat), "lon": jnp.where(flat, lon, lon_side)}
    at_one = jnp.where(flat, side, high)
    at_three = jnp.where(flat, high, side)
    pl.semaphore_signal(barrier, inc=1, device_id=peer_one, device_id_type=MESH)
    pl.semaphore_signal(barrier, inc=1, device_id=peer_two, device_id_type=MESH)
    pl.semaphore_signal(barrier, inc=1, device_id=peer_three, device_id_type=MESH)

    def z_peer(hop):
        return {"segment": seg, "lat": lax.rem(lat + 2 * hop, lat_total), "lon": lon}

    def greet_z(hop, carry):
        pl.semaphore_signal(barrier, inc=1, device_id=z_peer(hop), device_id_type=MESH)
        return carry

    lax.fori_loop(1, z_total, greet_z, 0)

    def own_w(layer):
        return (
            pltpu.make_async_copy(wqkv_hbm.at[layer], wqkv_s.at[core, layer], own_sem.at[layer, 0]),
            pltpu.make_async_copy(wout_hbm.at[layer], wout_s.at[core, layer], own_sem.at[layer, 1]),
        )

    def sent_w(layer):
        return (
            remote(wqkv_hbm.at[layer], wqkv_s.at[core, layer], w_send.at[layer, 0], w_recv.at[layer, 0], partner),
            remote(wout_hbm.at[layer], wout_s.at[core, layer], w_send.at[layer, 1], w_recv.at[layer, 1], partner),
        )

    def came_w(layer):
        other = 1 - core
        return (
            remote(wqkv_hbm.at[layer], wqkv_s.at[other, layer], w_send.at[layer, 0], w_recv.at[layer, 0], partner),
            remote(wout_hbm.at[layer], wout_s.at[other, layer], w_send.at[layer, 1], w_recv.at[layer, 1], partner),
        )

    for layer in range(MAXL):
        for copy in own_w(layer):
            copy.start()

    act_s[core] = jnp.broadcast_to((depth_ref[0] > 1).astype(F32), (8, 128))

    zeros = jnp.zeros((2, HALF, D), BF16)

    @pl.when(first)
    def _():
        xin[1] = zeros

        @pl.when(at_home)
        def _():
            xin[0, 0] = fields_ref[high, 1 - core]
            xin[0, 1] = fields_ref[high, core]
            stage[0] = fields_ref[1 - high, 1 - core]
            stage[1] = fields_ref[1 - high, core]

    @pl.when(jnp.logical_not(first))
    def _():
        gin[1] = zeros

        @pl.when(at_home)
        def _():
            gin[0, 0] = cot_ref[high, 1 - core]
            gin[0, 1] = cot_ref[high, core]
            stage[0] = cot_ref[1 - high, 1 - core]
            stage[1] = cot_ref[1 - high, core]

    @pl.when(jnp.logical_not(has_far))
    def _():
        for sl in range(2):
            halo[sl, 1] = jnp.zeros((HALF, D), BF16)
            rim_in[sl, 1] = jnp.zeros((HALF, 2 * D), BF16)

    pl.semaphore_wait(barrier, 6 + z_total - 1 + has_far.astype(jnp.int32))

    sent_act = remote(act_s.at[core], act_s.at[core], a_sem.at[0], a_sem.at[1], partner)
    came_act = remote(act_s.at[core], act_s.at[1 - core], a_sem.at[0], a_sem.at[1], partner)
    field_copy = remote(stage, xin.at[0], i_sem.at[0], i_sem.at[1], twin)
    target_copy = remote(stage, gin.at[0], i_sem.at[2], i_sem.at[3], twin)

    @pl.when(jnp.logical_and(at_home, first))
    def _():
        field_copy.start()

    @pl.when(jnp.logical_and(at_home, jnp.logical_not(first)))
    def _():
        target_copy.start()

    sent_act.start()
    for layer in range(MAXL):
        for copy in sent_w(layer):
            copy.start()

    def halo_near(sl):
        return remote(nrm.at[sl, 0], halo.at[sl, 0], h_send.at[sl, 0], h_recv.at[sl, 0], partner)

    def halo_far(sl):
        return remote(nrm.at[sl, 1], halo.at[sl, 1], h_send.at[sl, 1], h_recv.at[sl, 1], beyond)

    def rim_near(sl):
        return remote(rim.at[sl, 0], rim_in.at[sl, 0], r_send.at[sl, 0], r_recv.at[sl, 0], partner)

    def rim_far(sl):
        return remote(rim.at[sl, 1], rim_in.at[sl, 1], r_send.at[sl, 1], r_recv.at[sl, 1], beyond)

    def start_far(copy):
        @pl.when(has_far)
        def _():
            copy.start()

    def arrive_far(copy):
        @pl.when(has_far)
        def _():
            copy.wait_recv()

    def rows_left(unit):
        return remote(left.at[unit], left_in.at[unit], l_send.at[unit], l_recv.at[unit], partner)

    def rows_right(unit):
        return remote(right.at[unit, 1 - core], right_in.at[unit], t_send.at[unit], t_recv.at[unit], partner)

    def one_copy(unit):
        return remote(part_s.at[unit, 1 - at_one], one_in.at[unit], p_send.at[unit, 0], p_recv.at[unit, 0], peer_one)

    def two_copy(unit):
        return remote(one_s.at[unit, 1 - end], two_in.at[unit], p_send.at[unit, 1], p_recv.at[unit, 1], peer_two)

    def three_copy(unit):
        return remote(two_s.at[unit, 1 - at_three], three_in.at[unit], p_send.at[unit, 2], p_recv.at[unit, 2], peer_three)

    def col_copy(unit, hop):
        return remote(
            col_s.at[unit, lax.rem(z_at + hop, z_total)], col_in.at[unit, hop - 1],
            z_send.at[unit, hop - 1], z_recv.at[unit, hop - 1], z_peer(hop),
        )

    def fin_copy(layer):
        return remote(fin_s.at[1 - core, layer], fin_in.at[layer], f_send.at[layer], f_recv.at[layer], partner)

    def weight_term(unit):
        rows_left(unit).wait_recv()
        rows_right(unit).wait_recv()
        normed = jnp.concatenate([left[unit, 0], left_in[unit, 0]], axis=0)
        second = jnp.concatenate([left[unit, core], left_in[unit, core]], axis=0)
        grads_low = jnp.concatenate([right[unit, core], right_in[unit]], axis=0)
        shape = (z_total, 2, lon_total, D // (lat_total * lon_total), D)
        one = dot(normed, grads_low[:, :D], (0, 0)).reshape(shape)
        two = dot(second, grads_low[:, D:], (0, 0)).reshape(shape)
        both = jnp.concatenate([one, two], axis=3).astype(BF16)
        for x in range(2):
            for to in range(lon_total):
                to_side, to_end = (to + 1) // 2 % 2, to // 2
                part_s[unit, jnp.where(flat, to_side, x), to_end, jnp.where(flat, x, to_side)] = both[:, x, to]

        @pl.when(first)
        def _():
            one_copy(unit).start()

    def stage_two(unit):
        one_copy(unit).wait_recv()
        one_s[unit] = (part_s[unit, at_one].astype(F32) + one_in[unit].astype(F32)).astype(BF16)
        two_copy(unit).start()

    def stage_three(unit):
        two_copy(unit).wait_recv()
        two_s[unit] = (one_s[unit, end].astype(F32) + two_in[unit].astype(F32)).astype(BF16)
        three_copy(unit).start()

    def stage_four(unit):
        three_copy(unit).wait_recv()
        col_s[unit] = (two_s[unit, at_three].astype(F32) + three_in[unit].astype(F32)).astype(BF16)

        def send(hop, carry):
            col_copy(unit, hop).start()
            return carry

        lax.fori_loop(1, z_total, send, 0)

    def stage_five(unit):
        def add(hop, total):
            col_copy(unit, hop).wait_recv()
            return total + col_in[unit, hop - 1].astype(F32)

        owner, layer = unit // 2, unit % 2
        fin_s[owner, layer] = lax.fori_loop(1, z_total, add, col_s[unit, z_at].astype(F32))

        @pl.when(owner != core)
        def _():
            fin_copy(layer).start()

    act_copy = remote(outs.at[1], xin.at[0], x_send.at[0], x_recv.at[0], across)
    skip_copy = remote(outs.at[0], xin.at[1], x_send.at[1], x_recv.at[1], across)
    gact_copy = remote(handoff.at[0], gin.at[0], g_send.at[0], g_recv.at[0], across)
    gskip_copy = remote(handoff.at[1], gin.at[1], g_send.at[1], g_recv.at[1], across)

    def owner_of(sl):
        return {"segment": seg - core + sl, "lat": lat - high + core, "lon": lon}

    def out_copy(sl):
        return remote(outs.at[sl], out_in.at[high], o_send.at[sl], o_recv.at[high], owner_of(sl))

    def grad_copy(sl):
        return remote(grads.at[sl], grad_in.at[high], s_send.at[sl], s_recv.at[high], owner_of(sl))

    def hand_over(sl, copy, target, source):
        mine = jnp.logical_and(at_home, core == sl)

        @pl.when(mine)
        def _():
            target[high] = source[sl]

        @pl.when(jnp.logical_not(mine))
        def _():
            copy.start()

    key_at = lax.broadcasted_iota(jnp.int32, (1, TOK), 1)
    valid_far = jnp.where(key_at < HALF, 1.0, has_far.astype(F32))

    def rows_of(ref, index):
        return jnp.concatenate([ref[index, 0].astype(F32), ref[index, 1].astype(F32)], axis=0)

    def weights_ready(sl, layer):
        @pl.when(core == sl)
        def _():
            for copy in own_w(layer):
                copy.wait()

        @pl.when(core != sl)
        def _():
            for copy in came_w(layer):
                copy.wait_recv()

    @pl.when(jnp.logical_not(first))
    def _():
        act_copy.wait_recv()

    @pl.when(jnp.logical_and(first, jnp.logical_not(at_home)))
    def _():
        field_copy.wait_recv()

    stream_s[...] = rows_of(xin, 0)

    def forward(sl, carry):
        stream = stream_s[...]
        scaled, inverse = normalize(stream)
        normed = scaled.astype(BF16)
        xs[sl, 0] = scaled
        invs[sl, 0] = jnp.broadcast_to(inverse, (TOK, 128))
        left[2 * sl, 0] = normed
        weights_ready(sl, 0)
        qkv = dot(normed, wqkv_s[sl, 0], (1, 0))
        kv_low = qkv[:, D:].astype(BF16)
        kv_s[sl, 0] = kv_low

        def attend(layer, part, qkv, keys, valid):
            mixed = []
            for p in range(PAIRS):
                at = slice(128 * p, 128 * p + 128)
                q2 = split_heads(qkv[HALF * part : HALF * part + HALF, at])
                q2_s[sl, layer, p, TOK * part : TOK * part + TOK] = q2
                probs, mix = window_forward(q2, keys[:, at], keys[:, D + 128 * p : D + 128 * p + 128], valid)
                probs_s[sl, layer, p, TOK * part : TOK * part + TOK] = probs
                mixed.append(mix)
            return jnp.concatenate(mixed, axis=1)

        mixed = [None, None]
        streams = [None, None]
        scales = [None, None]
        for part in (1, 0):
            rows = slice(HALF * part, HALF * part + HALF)
            mixed[part] = attend(0, part, qkv, kv_low, None)
            streams[part] = stream[rows] + dot(mixed[part].astype(BF16), wout_s[sl, 0], (1, 0))
            scaled, inverse = normalize(streams[part])
            nrm[sl, part] = scaled.astype(BF16)
            xs[sl, 1, rows] = scaled
            invs[sl, 1, rows] = jnp.broadcast_to(inverse, (HALF, 128))
            scales[part] = scaled
            if part == 1:
                start_far(halo_far(sl))
            else:
                halo_near(sl).start()
        left[2 * sl, 1] = jnp.concatenate(mixed, axis=0).astype(BF16)
        stream = jnp.concatenate(streams, axis=0)

        normed = jnp.concatenate(scales, axis=0).astype(BF16)
        left[2 * sl + 1, 0] = normed
        weights_ready(sl, 1)

        rows_left(2 * sl).start()
        qkv = dot(normed, wqkv_s[sl, 1], (1, 0))
        for part in (0, 1):
            if part == 0:
                halo_near(sl).wait_recv()
            else:
                arrive_far(halo_far(sl))
            beside = dot(halo[sl, part], wqkv_s[sl, 1, :, D:], (1, 0))
            keys = jnp.concatenate([qkv[HALF * part : HALF * part + HALF, D:], beside], axis=0).astype(BF16)
            kv_s[sl, 1 + part] = keys
            mixed[part] = attend(1, part, qkv, keys, valid_far if part == 1 else None)
        mixed_low = jnp.concatenate(mixed, axis=0).astype(BF16)
        left[2 * sl + 1, 1] = mixed_low

        rows_left(2 * sl + 1).start()

        @pl.when(core != sl)
        def _():
            came_act.wait_recv()

        stream = stream + act_s[sl][0:1, 0:1] * dot(mixed_low, wout_s[sl, 1], (1, 0))
        for part in range(2):
            outs[sl, part] = stream[HALF * part : HALF * part + HALF].astype(BF16)
        hand_over(sl, out_copy(sl), out_in, outs)

        @pl.when(sl == 0)
        def _():
            @pl.when(first)
            def _():
                skip_copy.start()

            @pl.when(jnp.logical_not(first))
            def _():
                skip_copy.wait_recv()

            stream_s[...] = stream.astype(BF16).astype(F32) + rows_of(xin, 1)

        return carry

    lax.fori_loop(0, 2, forward, 0)

    @pl.when(first)
    def _():
        act_copy.start()
        gact_copy.wait_recv()

    @pl.when(jnp.logical_not(jnp.logical_or(first, at_home)))
    def _():
        target_copy.wait_recv()

    g_s[...] = rows_of(gin, 0)

    def backward(step, carry):
        sl = 1 - step
        g = g_s[...]
        glow = (g * act_s[sl][0:1, 0:1]).astype(BF16)
        right[2 * sl + 1, 1, :, D:] = glow
        gm = dot(glow, wout_s[sl, 1], (1, 1))
        gq, pairs = [None, None], [None, None]
        for part in (1, 0):
            rows = slice(TOK * part, TOK * part + TOK)
            q, k, v = [], [], []
            for p in range(PAIRS):
                at = slice(128 * p, 128 * p + 128)
                vat = slice(D + 128 * p, D + 128 * p + 128)
                found = window_backward(
                    split_heads(gm[HALF * part : HALF * part + HALF, at]), q2_s[sl, 1, p, rows],
                    kv_s[sl, 1 + part, :, at], kv_s[sl, 1 + part, :, vat], probs_s[sl, 1, p, rows],
                )
                q.append(join_heads(found[0]))
                k.append(found[1])
                v.append(found[2])
            gq[part] = jnp.concatenate(q, axis=1)
            pairs[part] = jnp.concatenate(k + v, axis=1)
            rim[sl, part] = pairs[part][HALF:].astype(BF16)
            if part == 1:
                start_far(rim_far(sl))
            else:
                rim_near(sl).start()
        query_low = jnp.concatenate(gq, axis=0).astype(BF16)
        right[2 * sl + 1, 0, :, :D] = query_low
        part = dot(query_low, wqkv_s[sl, 1, :, :D], (1, 1))

        @pl.when(step == 1)
        def _():
            weight_term(2)

        rim_near(sl).wait_recv()
        arrive_far(rim_far(sl))
        pairs_low = jnp.concatenate(
            [pairs[part][:HALF] + rim_in[sl, part].astype(F32) for part in range(2)], axis=0
        ).astype(BF16)
        right[2 * sl + 1, 0, :, D:] = pairs_low[:, :D]
        right[2 * sl + 1, 1, :, :D] = pairs_low[:, D:]

        rows_right(2 * sl + 1).start()
        part = part + dot(pairs_low, wqkv_s[sl, 1, :, D:], (1, 1))
        g = g + norm_back(xs[sl, 1], invs[sl, 1][:, 0:1], part)

        glow = g.astype(BF16)
        right[2 * sl, 1, :, D:] = glow
        gm = dot(glow, wout_s[sl, 0], (1, 1))
        gq, gk, gv = [], [], []
        for p in range(PAIRS):
            at = slice(128 * p, 128 * p + 128)
            vat = slice(D + 128 * p, D + 128 * p + 128)
            gm2 = jnp.concatenate([split_heads(gm[:HALF, at]), split_heads(gm[HALF:, at])], axis=0)
            q, k, v = window_backward(
                gm2, q2_s[sl, 0, p], kv_s[sl, 0, :, at], kv_s[sl, 0, :, vat], probs_s[sl, 0, p]
            )
            gq.append(jnp.concatenate([join_heads(q[:TOK]), join_heads(q[TOK:])], axis=0))
            gk.append(k)
            gv.append(v)
        low = jnp.concatenate(gq + gk + gv, axis=1).astype(BF16)
        right[2 * sl, 0] = low[:, : 2 * D]
        right[2 * sl, 1, :, :D] = low[:, 2 * D :]

        rows_right(2 * sl).start()
        part = dot(low, wqkv_s[sl, 0], (1, 1))
        g = g + norm_back(xs[sl, 0], invs[sl, 0][:, 0:1], part)
        for part in range(2):
            grads[sl, part] = g[HALF * part : HALF * part + HALF]
        @pl.when(step == 0)
        def _():
            hand_over(sl, grad_copy(sl), grad_in, grads)

        @pl.when(jnp.logical_not(first))
        def _():
            for part in range(2):
                handoff[1 - step, part] = g[HALF * part : HALF * part + HALF].astype(BF16)

            @pl.when(step == 0)
            def _():
                gskip_copy.start()

            @pl.when(step == 1)
            def _():
                gact_copy.start()

        @pl.when(step == 0)
        def _():
            @pl.when(first)
            def _():
                gskip_copy.wait_recv()

            g_s[...] = g + rows_of(gin, 1)

        weight_term(2 * sl + 1)
        return carry

    lax.fori_loop(0, 2, backward, 0)
    weight_term(0)

    @pl.when(jnp.logical_not(first))
    def _():
        for unit in (3, 2, 1, 0):
            one_copy(unit).start()

    hand_over(0, grad_copy(0), grad_in, grads)
    stage_two(3)
    stage_two(2)
    stage_three(3)
    stage_two(1)
    stage_three(2)
    stage_four(3)
    stage_three(1)
    stage_four(2)
    stage_two(0)
    stage_four(1)
    stage_five(3)
    stage_five(2)
    stage_three(0)
    stage_five(1)
    stage_four(0)
    stage_five(0)

    for pair in range(2):
        came = jnp.logical_not(jnp.logical_and(at_home, high == pair))

        @pl.when(came)
        def _():
            remote(outs.at[0], out_in.at[pair], o_send.at[0], o_recv.at[pair], partner).wait_recv()
            remote(grads.at[0], grad_in.at[pair], s_send.at[0], s_recv.at[pair], partner).wait_recv()

        out_ref[pair, 0] = out_in[pair, 1 - high]
        out_ref[pair, 1] = out_in[pair, high]
        grad_ref[pair, 0] = grad_in[pair, 1 - high]
        grad_ref[pair, 1] = grad_in[pair, high]

    piece = D // (lat_total * lon_total)
    for layer in range(MAXL):
        fin_copy(layer).wait_recv()
        mine, came = fin_s[core, layer], fin_in[layer]
        first_half = jnp.where(core == 0, mine, came)
        second_half = jnp.where(core == 0, came, mine)
        qkv_ref[layer, :, :D] = first_half[:piece]
        qkv_ref[layer, :, D : 2 * D] = first_half[piece:]
        qkv_ref[layer, :, 2 * D :] = second_half[:piece]
        wo_ref[layer] = second_half[piece:]

    sent_act.wait_send()

    for layer in range(MAXL):
        for copy in sent_w(layer):
            copy.wait_send()
        fin_copy(layer).wait_send()
    for unit in range(4):
        rows_left(unit).wait_send()
        rows_right(unit).wait_send()

        one_copy(unit).wait_send()
        two_copy(unit).wait_send()
        three_copy(unit).wait_send()

        def sent(hop, carry):
            col_copy(unit, hop).wait_send()
            return carry

        lax.fori_loop(1, z_total, sent, 0)
    for sl in range(2):
        @pl.when(jnp.logical_not(jnp.logical_and(at_home, core == sl)))
        def _():
            out_copy(sl).wait_send()
            grad_copy(sl).wait_send()

        halo_near(sl).wait_send()
        rim_near(sl).wait_send()

        @pl.when(has_far)
        def _():
            halo_far(sl).wait_send()
            rim_far(sl).wait_send()

    @pl.when(jnp.logical_and(at_home, first))
    def _():
        field_copy.wait_send()

    @pl.when(jnp.logical_and(at_home, jnp.logical_not(first)))
    def _():
        target_copy.wait_send()

    @pl.when(first)
    def _():
        act_copy.wait_send()
        skip_copy.wait_send()

    @pl.when(jnp.logical_not(first))
    def _():
        gact_copy.wait_send()
        gskip_copy.wait_send()


def network(fields, cotangent, depths, w_qkv, w_out, lat_total, lon_total):
    piece = 2 * D // (lat_total * lon_total)
    z_total = lat_total // 2
    vmem = pl.BlockSpec(memory_space=pltpu.VMEM)
    hbm = pl.BlockSpec(memory_space=pl.ANY)
    dma = pltpu.SemaphoreType.DMA
    scratch = [
        pltpu.VMEM((2, MAXL, D, 3 * D), BF16),
        pltpu.VMEM((2, MAXL, D, D), BF16),
        pltpu.VMEM((2, 8, 128), F32),
        pltpu.VMEM((2, HALF, D), BF16),
        pltpu.VMEM((2, 2, HALF, D), BF16),
        pltpu.VMEM((2, 2, HALF, D), BF16),
        pltpu.VMEM((TOK, D), F32),
        pltpu.VMEM((TOK, D), F32),
        pltpu.VMEM((2, 2, HALF, D), BF16),
        pltpu.VMEM((2, 2, HALF, D), BF16),
        pltpu.VMEM((2, 2, HALF, D), F32),
        pltpu.VMEM((2, 2, HALF, D), F32),
        pltpu.VMEM((2, 2, HALF, D), BF16),
        pltpu.VMEM((2, 2, HALF, D), BF16),
        pltpu.VMEM((2, 2, HALF, D), BF16),
        pltpu.VMEM((2, 2, HALF, 2 * D), BF16),
        pltpu.VMEM((2, 2, HALF, 2 * D), BF16),
        pltpu.VMEM((2, MAXL, TOK, D), F32),
        pltpu.VMEM((2, MAXL, TOK, 128), F32),
        pltpu.VMEM((2, MAXL, PAIRS, 2 * TOK, TOK), F32),
        pltpu.VMEM((2, MAXL, PAIRS, 2 * TOK, 128), BF16),
        pltpu.VMEM((2, 3, TOK, 2 * D), BF16),
        pltpu.VMEM((4, 2, TOK, D), BF16),
        pltpu.VMEM((4, 2, TOK, D), BF16),
        pltpu.VMEM((4, 2, TOK, 2 * D), BF16),
        pltpu.VMEM((4, TOK, 2 * D), BF16),
        pltpu.VMEM((4, 2, 2, 2, z_total, piece, D), BF16),
        pltpu.VMEM((4, 2, 2, z_total, piece, D), BF16),
        pltpu.VMEM((4, 2, 2, z_total, piece, D), BF16),
        pltpu.VMEM((4, 2, z_total, piece, D), BF16),
        pltpu.VMEM((4, 2, z_total, piece, D), BF16),
        pltpu.VMEM((4, z_total, piece, D), BF16),
        pltpu.VMEM((4, z_total, piece, D), BF16),
        pltpu.VMEM((4, z_total - 1, piece, D), BF16),
        pltpu.VMEM((2, MAXL, piece, D), F32),
        pltpu.VMEM((MAXL, piece, D), F32),
        dma((MAXL, 2)),
        dma((MAXL, 2)),
        dma((MAXL, 2)),
        dma((2,)),
        dma((4,)),
        dma((2,)),
        dma((2,)),
        dma((2,)),
        dma((2,)),
        dma((2,)),
        dma((2,)),
        dma((2,)),
        dma((2,)),
        dma((2, 2)),
        dma((2, 2)),
        dma((2, 2)),
        dma((2, 2)),
        dma((4,)),
        dma((4,)),
        dma((4,)),
        dma((4,)),
        dma((4, 3)),
        dma((4, 3)),
        dma((4, z_total - 1)),
        dma((4, z_total - 1)),
        dma((MAXL,)),
        dma((MAXL,)),
    ]
    return pl.pallas_call(
        partial(body, lat_total, lon_total),
        out_shape=(
            jax.ShapeDtypeStruct((2, 2, HALF, D), BF16),
            jax.ShapeDtypeStruct((2, 2, HALF, D), F32),
            jax.ShapeDtypeStruct((MAXL, piece // 2, 3 * D), F32),
            jax.ShapeDtypeStruct((MAXL, piece // 2, D), F32),
        ),
        in_specs=[vmem, vmem, pl.BlockSpec(memory_space=pltpu.SMEM), hbm, hbm],
        out_specs=(vmem, vmem, vmem, vmem),
        scratch_shapes=scratch,
        compiler_params=pltpu.CompilerParams(
            collective_id=0, has_side_effects=True, vmem_limit_bytes=56 * 1024 * 1024
        ),
        name="network",
    )(fields, cotangent, depths, w_qkv, w_out)


def to_rows(cells):
    shaped = cells.reshape(2, WIN_LEV, 2, 6, WIN_LON, D).transpose(0, 2, 1, 3, 4, 5)
    return shaped.reshape(2, 2, HALF, D)


def from_rows(rows):
    shaped = rows.reshape(2, 2, WIN_LEV, 6, WIN_LON, D).transpose(0, 2, 1, 3, 4, 5)
    return shaped.reshape(1, 2 * WIN_LEV, 12, WIN_LON, D)


def local(fields, cotangent, depths, w_qkv, w_out):
    out_rows, grad_rows, qkv_grad, out_grad = network(
        to_rows(fields), to_rows(cotangent), depths, w_qkv[0], w_out[0],
        lax.axis_size("lat"), lax.axis_size("lon"),
    )
    return (
        from_rows(out_rows),
        from_rows(grad_rows),
        qkv_grad[None],
        out_grad[None],
    )


def solution(mesh):
    placed = (
        P(None, "lat", "lon", None),
        P(None, "lat", "lon", None),
        P("segment"),
        P("segment", None, None, None),
        P("segment", None, None, None),
    )
    return jax.shard_map(
        local,
        mesh=mesh,
        in_specs=placed,
        out_specs=(
            P("segment", None, "lat", "lon", None),
            P("segment", None, "lat", "lon", None),
            P("segment", None, ("lat", "lon"), None),
            P("segment", None, ("lat", "lon"), None),
        ),
        check_vma=False,
    )
```

time: 172 us -> 147 us (0.85)
  Pallas kernels: 157 us -> 132 us
    pallas_call x1, Pallas kernels: 157 us -> 132 us  [network(): pl.pallas_call(partial(body, lat_total, lon_total), out_shape=(jax.ShapeD...]
    broadcast_in_dim x3 -> x0, local copies, waits for them, and re-layouts: 3.51 us -> none  [the longest x1 1.54 us: local(): shaped[None, :, :, :3 * D]]
    reshape x2 -> x6, local copies, waits for them, and re-layouts: 1.43 us -> 4.26 us  [the longest x4 2.76 us: to_rows(): cells.reshape(2, WIN_LEV, 2, 6, WIN_LON, D).transpose(0, 2, 1, 3, 4, 5)]
where the time goes in v3:
time: 147 us; the launch traced here: 145 us
  Pallas kernels  132 us (90%)
  local copies, waits for them, and re-layouts  11.1 us (8%)
    pallas_call x1, Pallas kernels, network(): pl.pallas_call(partial(body, lat_total, lon_total), out_shape=(jax.ShapeD...  132 us

profile of v3, /device:TPU:8, one launch (start us, length us, event | category | flops | bytes accessed | tf_op | source)
XLA Modules:
  0.0 144.6 jit_solution(4801700115466300918)
XLA Ops:
  1.3 1.1 reshape.32
  2.4 0.3 copy.19
  2.7 0.7 copy.21.fields_ref
  3.4 1.1 reshape.34
  4.5 0.3 copy.20
  4.8 0.7 copy.22.cot_ref
  5.6 132.1 %network.1 = (bf16[2,2,72,512]{3,2,1,0:T(8,128)(2,1)}, f32[2,2,72,512]{3,2,1,0:T(8,128)}, f32[2,8,1536]{2,1,0:T(8,128)}, f32[2,8,512]{2,1,0:T(8,128)}) custom-call(bf16[2,2,72,512]{3,2,1,0:T(8,128)(2,1)} %copy.21.fields_ref, bf16[2,2,72,512]{3,2,1,0:T(8,128)(2,1)} %copy.22.cot_ref, s32[1]{0:T(128)S(6)} %copy.29.depth_ref, bf16[2,512,1536]{2,1,0:T(8,128)(2,1)} %bitcast.24, ...), custom_call_target="tpu_custom_call" | custom-call | tf_op jit(solution)/shard_map/network/pallas_call | solution.py:727
  137.7 0.0 copy-start
  137.7 0.0 copy-start.1
  137.7 1.2 copy.23
  138.9 0.2 copy.24
  139.2 0.8 reshape.37
  140.0 1.5 %copy.25 = f32[2,2,72,512]{3,1,2,0:T(2,128)S(1)} copy(f32[2,2,72,512]{3,2,1,0:T(8,128)} %get-tuple-element.9) | data formatting | bytes 1179648 | tf_op jit(solution)/shard_map/network/pallas_call | solution.py:727
  141.5 0.5 copy.26
  142.0 1.3 reshape.39
  143.3 0.0 copy-done
  143.3 0.6 copy.30
  143.9 0.0 copy-done.1
  144.0 0.6 copy.31
Async XLA Ops:
  137.7 5.6 %copy-start = (f32[2,8,1536]{2,1,0:T(8,128)S(1)}, f32[2,8,1536]{2,1,0:T(8,128)}, u32[]{:S(2)}) copy-start(f32[2,8,1536]{2,1,0:T(8,128)} %get-tuple-element.10) | copy-start | bytes 294916
  137.7 6.3 %copy-start.1 = (f32[2,8,512]{2,1,0:T(8,128)S(1)}, f32[2,8,512]{2,1,0:T(8,128)}, u32[]{:S(2)}) copy-start(f32[2,8,512]{2,1,0:T(8,128)} %get-tuple-element.11) | copy-start | bytes 98308

commit v4 on v3

--- a/solution.py
+++ b/solution.py
@@ -49,21 +49,46 @@
 
 
 def window_forward(q2, k, v, valid):
-    exponent = jnp.exp(dot(q2, k, (1, 1)) * (HS ** -0.5))
+    exponent = jnp.exp(dot(k, q2, (1, 1)) * (HS ** -0.5))
     if valid is not None:
         exponent = exponent * valid
-    probs = exponent * (1.0 / jnp.sum(exponent, axis=-1, keepdims=True))
-    return probs, join_heads(dot(probs.astype(BF16), v, (1, 0)))
+    probs = exponent * (1.0 / jnp.sum(exponent, axis=0, keepdims=True))
+    return probs, join_heads(dot(probs.astype(BF16), v, (0, 0)))
 
 
 def window_backward(gm2, q2, k, v, probs):
-    grad_probs = dot(gm2, v, (1, 1))
-    inner = jnp.sum(probs * grad_probs, axis=-1, keepdims=True)
+    grad_probs = dot(v, gm2, (1, 1))
+    inner = jnp.sum(probs * grad_probs, axis=0, keepdims=True)
     grad_scores = (probs * (grad_probs - inner) * (HS ** -0.5)).astype(BF16)
-    gq = dot(grad_scores, k, (1, 0))
-    gk = dot(grad_scores, q2, (0, 0))
-    gv = dot(probs.astype(BF16), gm2, (0, 0))
+    gq = join_heads(dot(grad_scores, k, (0, 0)))
+    gk = dot(grad_scores, q2, (1, 0))
+    gv = dot(probs.astype(BF16), gm2, (1, 0))
     return gq, gk, gv
+
+
+def picker(pair, shape, row_dim):
+    rows = lax.broadcasted_iota(jnp.int32, shape, row_dim)
+    cells = lax.broadcasted_iota(jnp.int32, shape, 1 - row_dim)
+    return jnp.where(cells == 4 * (rows // 2) + 2 * pair + rows % 2, 1.0, 0.0)
+
+
+def take_rows(ref, pair, half):
+    cells = [ref[6 * half + row, col].astype(F32) for row in range(6) for col in range(WIN_LON)]
+    cells = jnp.concatenate(cells, axis=0).astype(BF16)
+    return dot(picker(pair, (HALF, TOK), 0).astype(BF16), cells, (1, 0)).astype(BF16)
+
+
+def put_rows(ref, half, pairs):
+    cells = 0.0
+    for pair in range(2):
+        cells = cells + lax.dot_general(
+            picker(pair, (TOK, HALF), 1), pairs[pair], (((1,), (0,)), ((), ())),
+            precision=lax.Precision.HIGHEST, preferred_element_type=F32,
+        )
+    for row in range(6):
+        for col in range(WIN_LON):
+            at = 4 * (WIN_LON * row + col)
+            ref[6 * half + row, col] = cells[at : at + 4].astype(ref.dtype)
 
 
 def body(
@@ -112,15 +137,10 @@
     side, end = lax.rem((lon + 1) // 2, 2), lon // 2
     lon_side = lon + 1 - 2 * lax.rem(lon, 2)
     lon_end = lon_total - 1 - lon
-    flat = core == 0
-    peer_one = {"segment": seg, "lat": jnp.where(flat, lat, twin_lat), "lon": jnp.where(flat, lon_side, lon)}
-    peer_two = {"segment": seg, "lat": lat, "lon": lon_end}
-    peer_three = {"segment": seg, "lat": jnp.where(flat, twin_lat, lat), "lon": jnp.where(flat, lon, lon_side)}
-    at_one = jnp.where(flat, side, high)
-    at_three = jnp.where(flat, high, side)
-    pl.semaphore_signal(barrier, inc=1, device_id=peer_one, device_id_type=MESH)
-    pl.semaphore_signal(barrier, inc=1, device_id=peer_two, device_id_type=MESH)
-    pl.semaphore_signal(barrier, inc=1, device_id=peer_three, device_id_type=MESH)
+    for peer_lon in (lon_side, lon_end):
+        to = {"segment": seg, "lat": lat, "lon": peer_lon}
+        pl.semaphore_signal(barrier, inc=1, device_id=to, device_id_type=MESH)
+    pl.semaphore_signal(barrier, inc=1, device_id=twin, device_id_type=MESH)
 
     def z_peer(hop):
         return {"segment": seg, "lat": lax.rem(lat + 2 * hop, lat_total), "lon": lon}
@@ -164,10 +184,10 @@
 
         @pl.when(at_home)
         def _():
-            xin[0, 0] = fields_ref[high, 1 - core]
-            xin[0, 1] = fields_ref[high, core]
-            stage[0] = fields_ref[1 - high, 1 - core]
-            stage[1] = fields_ref[1 - high, core]
+            xin[0, 0] = take_rows(fields_ref, high, 1 - core)
+            xin[0, 1] = take_rows(fields_ref, high, core)
+            stage[0] = take_rows(fields_ref, 1 - high, 1 - core)
+            stage[1] = take_rows(fields_ref, 1 - high, core)
 
     @pl.when(jnp.logical_not(first))
     def _():
@@ -175,10 +195,10 @@
 
         @pl.when(at_home)
         def _():
-            gin[0, 0] = cot_ref[high, 1 - core]
-            gin[0, 1] = cot_ref[high, core]
-            stage[0] = cot_ref[1 - high, 1 - core]
-            stage[1] = cot_ref[1 - high, core]
+            gin[0, 0] = take_rows(cot_ref, high, 1 - core)
+            gin[0, 1] = take_rows(cot_ref, high, core)
+            stage[0] = take_rows(cot_ref, 1 - high, 1 - core)
+            stage[1] = take_rows(cot_ref, 1 - high, core)
 
     @pl.when(jnp.logical_not(has_far))
     def _():
@@ -234,14 +254,35 @@
     def rows_right(unit):
         return remote(right.at[unit, 1 - core], right_in.at[unit], t_send.at[unit], t_recv.at[unit], partner)
 
-    def one_copy(unit):
-        return remote(part_s.at[unit, 1 - at_one], one_in.at[unit], p_send.at[unit, 0], p_recv.at[unit, 0], peer_one)
-
-    def two_copy(unit):
-        return remote(one_s.at[unit, 1 - end], two_in.at[unit], p_send.at[unit, 1], p_recv.at[unit, 1], peer_two)
-
-    def three_copy(unit):
-        return remote(two_s.at[unit, 1 - at_three], three_in.at[unit], p_send.at[unit, 2], p_recv.at[unit, 2], peer_three)
+    def order_of(unit, tile):
+        if tile == 0:
+            return core == 1, core == 0
+        return jnp.logical_and(core == 1, unit == 0), jnp.logical_and(core == 1, lax.rem(unit, 2) == 1)
+
+    def arranged(unit, tile, of_side, of_end, of_twin):
+        twin_first, side_first = order_of(unit, tile)
+        if tile == 0:
+            return jnp.where(twin_first, of_twin, of_side), of_end, jnp.where(twin_first, of_side, of_twin)
+        one = jnp.where(twin_first, of_twin, jnp.where(side_first, of_side, of_end))
+        return one, jnp.where(side_first, of_end, of_side), jnp.where(twin_first, of_end, of_twin)
+
+    def pairs_of(unit, tile):
+        ats = arranged(unit, tile, side, end, high)
+        lats = arranged(unit, tile, lat, lat, twin_lat)
+        lons = arranged(unit, tile, lon_side, lon_end, lon)
+        return [(at, {"segment": seg, "lat": a, "lon": b}) for at, a, b in zip(ats, lats, lons)]
+
+    def pair_copy(unit, tile, level):
+        at, peer = pairs_of(unit, tile)[level]
+        source = (part_s, one_s, two_s)[level].at[unit, tile, 1 - at]
+        target = (one_in, two_in, three_in)[level].at[unit, tile]
+        return remote(source, target, p_send.at[unit, tile, level], p_recv.at[unit, tile, level], peer)
+
+    def pair_sum(unit, tile, level):
+        at = pairs_of(unit, tile)[level][0]
+        pair_copy(unit, tile, level).wait_recv()
+        kept = (part_s, one_s, two_s)[level][unit, tile, at]
+        return (kept.astype(F32) + (one_in, two_in, three_in)[level][unit, tile].astype(F32)).astype(BF16)
 
     def col_copy(unit, hop):
         return remote(
@@ -259,37 +300,35 @@
         second = jnp.concatenate([left[unit, core], left_in[unit, core]], axis=0)
         grads_low = jnp.concatenate([right[unit, core], right_in[unit]], axis=0)
         shape = (z_total, 2, lon_total, D // (lat_total * lon_total), D)
-        one = dot(normed, grads_low[:, :D], (0, 0)).reshape(shape)
-        two = dot(second, grads_low[:, D:], (0, 0)).reshape(shape)
-        both = jnp.concatenate([one, two], axis=3).astype(BF16)
-        for x in range(2):
-            for to in range(lon_total):
-                to_side, to_end = (to + 1) // 2 % 2, to // 2
-                part_s[unit, jnp.where(flat, to_side, x), to_end, jnp.where(flat, x, to_side)] = both[:, x, to]
-
-        @pl.when(first)
-        def _():
-            one_copy(unit).start()
+        for tile in range(2):
+            term = dot(second if tile else normed, grads_low[:, D * tile : D * tile + D], (0, 0)).reshape(shape)
+            term = jnp.concatenate([term[..., : D // 2], term[..., D // 2 :]], axis=3).astype(BF16)
+            for x in range(2):
+                for to in range(lon_total):
+                    to_side, to_end = (to + 1) // 2 % 2, to // 2
+                    one, two, three = arranged(unit, tile, to_side, to_end, x)
+                    part_s[unit, tile, one, two, three] = term[:, x, to]
+
+            @pl.when(first)
+            def _():
+                pair_copy(unit, tile, 0).start()
 
     def stage_two(unit):
-        one_copy(unit).wait_recv()
-        one_s[unit] = (part_s[unit, at_one].astype(F32) + one_in[unit].astype(F32)).astype(BF16)
-        two_copy(unit).start()
+        for tile in range(2):
+            one_s[unit, tile] = pair_sum(unit, tile, 0)
+            pair_copy(unit, tile, 1).start()
 
     def stage_three(unit):
-        two_copy(unit).wait_recv()
-        two_s[unit] = (one_s[unit, end].astype(F32) + two_in[unit].astype(F32)).astype(BF16)
-        three_copy(unit).start()
+        for tile in range(2):
+            two_s[unit, tile] = pair_sum(unit, tile, 1)
+            pair_copy(unit, tile, 2).start()
 
     def stage_four(unit):
-        three_copy(unit).wait_recv()
-        col_s[unit] = (two_s[unit, at_three].astype(F32) + three_in[unit].astype(F32)).astype(BF16)
-
-        def send(hop, carry):
+        for tile in range(2):
+            col_s[unit, :, tile] = pair_sum(unit, tile, 2)
+
+        for hop in sorted(range(1, z_total), key=lambda hop: -min(hop, z_total - hop)):
             col_copy(unit, hop).start()
-            return carry
-
-        lax.fori_loop(1, z_total, send, 0)
 
     def stage_five(unit):
         def add(hop, total):
@@ -328,7 +367,7 @@
         def _():
             copy.start()
 
-    key_at = lax.broadcasted_iota(jnp.int32, (1, TOK), 1)
+    key_at = lax.broadcasted_iota(jnp.int32, (TOK, 1), 0)
     valid_far = jnp.where(key_at < HALF, 1.0, has_far.astype(F32))
 
     def rows_of(ref, index):
@@ -374,7 +413,7 @@
                 q2 = split_heads(qkv[HALF * part : HALF * part + HALF, at])
                 q2_s[sl, layer, p, TOK * part : TOK * part + TOK] = q2
                 probs, mix = window_forward(q2, keys[:, at], keys[:, D + 128 * p : D + 128 * p + 128], valid)
-                probs_s[sl, layer, p, TOK * part : TOK * part + TOK] = probs
+                probs_s[sl, layer, p, part] = probs
                 mixed.append(mix)
             return jnp.concatenate(mixed, axis=1)
 
@@ -468,9 +507,9 @@
                 vat = slice(D + 128 * p, D + 128 * p + 128)
                 found = window_backward(
                     split_heads(gm[HALF * part : HALF * part + HALF, at]), q2_s[sl, 1, p, rows],
-                    kv_s[sl, 1 + part, :, at], kv_s[sl, 1 + part, :, vat], probs_s[sl, 1, p, rows],
+                    kv_s[sl, 1 + part, :, at], kv_s[sl, 1 + part, :, vat], probs_s[sl, 1, p, part],
                 )
-                q.append(join_heads(found[0]))
+                q.append(found[0])
                 k.append(found[1])
                 v.append(found[2])
             gq[part] = jnp.concatenate(q, axis=1)
@@ -507,11 +546,16 @@
         for p in range(PAIRS):
             at = slice(128 * p, 128 * p + 128)
             vat = slice(D + 128 * p, D + 128 * p + 128)
-            gm2 = jnp.concatenate([split_heads(gm[:HALF, at]), split_heads(gm[HALF:, at])], axis=0)
-            q, k, v = window_backward(
-                gm2, q2_s[sl, 0, p], kv_s[sl, 0, :, at], kv_s[sl, 0, :, vat], probs_s[sl, 0, p]
-            )
-            gq.append(jnp.concatenate([join_heads(q[:TOK]), join_heads(q[TOK:])], axis=0))
+            found = [
+                window_backward(
+                    split_heads(gm[HALF * part : HALF * part + HALF, at]), q2_s[sl, 0, p, TOK * part : TOK * part + TOK],
+                    kv_s[sl, 0, :, at], kv_s[sl, 0, :, vat], probs_s[sl, 0, p, part],
+                )
+                for part in range(2)
+            ]
+            gq.append(jnp.concatenate([found[0][0], found[1][0]], axis=0))
+            k = found[0][1] + found[1][1]
+            v = found[0][2] + found[1][2]
             gk.append(k)
             gv.append(v)
         low = jnp.concatenate(gq + gk + gv, axis=1).astype(BF16)
@@ -557,7 +601,8 @@
     @pl.when(jnp.logical_not(first))
     def _():
         for unit in (3, 2, 1, 0):
-            one_copy(unit).start()
+            for tile in range(2):
+                pair_copy(unit, tile, 0).start()
 
     hand_over(0, grad_copy(0), grad_in, grads)
     stage_two(3)
@@ -574,21 +619,21 @@
     stage_five(2)
     stage_three(0)
     stage_five(1)
+    for pair in range(2):
+        came = jnp.logical_not(jnp.logical_and(at_home, high == pair))
+
+        @pl.when(came)
+        def _():
+            remote(outs.at[0], out_in.at[pair], o_send.at[0], o_recv.at[pair], partner).wait_recv()
+            remote(grads.at[0], grad_in.at[pair], s_send.at[0], s_recv.at[pair], partner).wait_recv()
+
+    for half in range(2):
+        index = (1 - high) if half == 0 else high
+        put_rows(out_ref, half, [out_in[pair, index].astype(F32) for pair in range(2)])
+        put_rows(grad_ref, half, [grad_in[pair, index] for pair in range(2)])
+
     stage_four(0)
     stage_five(0)
-
-    for pair in range(2):
-        came = jnp.logical_not(jnp.logical_and(at_home, high == pair))
-
-        @pl.when(came)
-        def _():
-            remote(outs.at[0], out_in.at[pair], o_send.at[0], o_recv.at[pair], partner).wait_recv()
-            remote(grads.at[0], grad_in.at[pair], s_send.at[0], s_recv.at[pair], partner).wait_recv()
-
-        out_ref[pair, 0] = out_in[pair, 1 - high]
-        out_ref[pair, 1] = out_in[pair, high]
-        grad_ref[pair, 0] = grad_in[pair, 1 - high]
-        grad_ref[pair, 1] = grad_in[pair, high]
 
     piece = D // (lat_total * lon_total)
     for layer in range(MAXL):
@@ -596,10 +641,13 @@
         mine, came = fin_s[core, layer], fin_in[layer]
         first_half = jnp.where(core == 0, mine, came)
         second_half = jnp.where(core == 0, came, mine)
-        qkv_ref[layer, :, :D] = first_half[:piece]
-        qkv_ref[layer, :, D : 2 * D] = first_half[piece:]
-        qkv_ref[layer, :, 2 * D :] = second_half[:piece]
-        wo_ref[layer] = second_half[piece:]
+        for side_at in range(2):
+            at = D // 2 * side_at
+            rows = slice(piece * side_at, piece * side_at + piece)
+            qkv_ref[layer, :, at : at + D // 2] = first_half[0, rows]
+            qkv_ref[layer, :, D + at : D + at + D // 2] = first_half[1, rows]
+            qkv_ref[layer, :, 2 * D + at : 2 * D + at + D // 2] = second_half[0, rows]
+            wo_ref[layer, :, at : at + D // 2] = second_half[1, rows]
 
     sent_act.wait_send()
 
@@ -611,9 +659,9 @@
         rows_left(unit).wait_send()
         rows_right(unit).wait_send()
 
-        one_copy(unit).wait_send()
-        two_copy(unit).wait_send()
-        three_copy(unit).wait_send()
+        for tile in range(2):
+            for level in range(3):
+                pair_copy(unit, tile, level).wait_send()
 
         def sent(hop, carry):
             col_copy(unit, hop).wait_send()
@@ -679,23 +727,23 @@
         pltpu.VMEM((2, 2, HALF, 2 * D), BF16),
         pltpu.VMEM((2, MAXL, TOK, D), F32),
         pltpu.VMEM((2, MAXL, TOK, 128), F32),
-        pltpu.VMEM((2, MAXL, PAIRS, 2 * TOK, TOK), F32),
+        pltpu.VMEM((2, MAXL, PAIRS, 2, TOK, TOK), F32),
         pltpu.VMEM((2, MAXL, PAIRS, 2 * TOK, 128), BF16),
         pltpu.VMEM((2, 3, TOK, 2 * D), BF16),
         pltpu.VMEM((4, 2, TOK, D), BF16),
         pltpu.VMEM((4, 2, TOK, D), BF16),
         pltpu.VMEM((4, 2, TOK, 2 * D), BF16),
         pltpu.VMEM((4, TOK, 2 * D), BF16),
-        pltpu.VMEM((4, 2, 2, 2, z_total, piece, D), BF16),
-        pltpu.VMEM((4, 2, 2, z_total, piece, D), BF16),
-        pltpu.VMEM((4, 2, 2, z_total, piece, D), BF16),
-        pltpu.VMEM((4, 2, z_total, piece, D), BF16),
-        pltpu.VMEM((4, 2, z_total, piece, D), BF16),
-        pltpu.VMEM((4, z_total, piece, D), BF16),
-        pltpu.VMEM((4, z_total, piece, D), BF16),
-        pltpu.VMEM((4, z_total - 1, piece, D), BF16),
-        pltpu.VMEM((2, MAXL, piece, D), F32),
-        pltpu.VMEM((MAXL, piece, D), F32),
+        pltpu.VMEM((4, 2, 2, 2, 2, z_total, piece, D // 2), BF16),
+        pltpu.VMEM((4, 2, 2, 2, z_total, piece, D // 2), BF16),
+        pltpu.VMEM((4, 2, 2, 2, z_total, piece, D // 2), BF16),
+        pltpu.VMEM((4, 2, 2, z_total, piece, D // 2), BF16),
+        pltpu.VMEM((4, 2, 2, z_total, piece, D // 2), BF16),
+        pltpu.VMEM((4, 2, z_total, piece, D // 2), BF16),
+        pltpu.VMEM((4, z_total, 2, piece, D // 2), BF16),
+        pltpu.VMEM((4, z_total - 1, 2, piece, D // 2), BF16),
+        pltpu.VMEM((2, MAXL, 2, piece, D // 2), F32),
+        pltpu.VMEM((MAXL, 2, piece, D // 2), F32),
         dma((MAXL, 2)),
         dma((MAXL, 2)),
         dma((MAXL, 2)),
@@ -717,8 +765,8 @@
         dma((4,)),
         dma((4,)),
         dma((4,)),
-        dma((4, 3)),
-        dma((4, 3)),
+        dma((4, 2, 3)),
+        dma((4, 2, 3)),
         dma((4, z_total - 1)),
         dma((4, z_total - 1)),
         dma((MAXL,)),
@@ -727,8 +775,8 @@
     return pl.pallas_call(
         partial(body, lat_total, lon_total),
         out_shape=(
-            jax.ShapeDtypeStruct((2, 2, HALF, D), BF16),
-            jax.ShapeDtypeStruct((2, 2, HALF, D), F32),
+            jax.ShapeDtypeStruct(fields.shape, BF16),
+            jax.ShapeDtypeStruct(fields.shape, F32),
             jax.ShapeDtypeStruct((MAXL, piece // 2, 3 * D), F32),
             jax.ShapeDtypeStruct((MAXL, piece // 2, D), F32),
         ),
@@ -742,24 +790,14 @@
     )(fields, cotangent, depths, w_qkv, w_out)
 
 
-def to_rows(cells):
-    shaped = cells.reshape(2, WIN_LEV, 2, 6, WIN_LON, D).transpose(0, 2, 1, 3, 4, 5)
-    return shaped.reshape(2, 2, HALF, D)
-
-
-def from_rows(rows):
-    shaped = rows.reshape(2, 2, WIN_LEV, 6, WIN_LON, D).transpose(0, 2, 1, 3, 4, 5)
-    return shaped.reshape(1, 2 * WIN_LEV, 12, WIN_LON, D)
-
-
 def local(fields, cotangent, depths, w_qkv, w_out):
     out_rows, grad_rows, qkv_grad, out_grad = network(
-        to_rows(fields), to_rows(cotangent), depths, w_qkv[0], w_out[0],
+        fields.transpose(1, 2, 0, 3), cotangent.transpose(1, 2, 0, 3), depths, w_qkv[0], w_out[0],
         lax.axis_size("lat"), lax.axis_size("lon"),
     )
     return (
-        from_rows(out_rows),
-        from_rows(grad_rows),
+        out_rows.transpose(2, 0, 1, 3)[None],
+        grad_rows.transpose(2, 0, 1, 3)[None],
         qkv_grad[None],
         out_grad[None],
     )

time: 147 us -> 138 us (0.939); the launches traced: 145 us -> 137 us
  local copies, waits for them, and re-layouts: 11.1 us -> 6.61 us
  Pallas kernels: 132 us -> 129 us
    reshape x8 -> x0, local copies, waits for them, and re-layouts: 6.4 us -> none  [the longest x4 2.76 us: to_rows(): cells.reshape(2, WIN_LEV, 2, 6, WIN_LON, D).transpose(0, 2, 1, 3, 4, 5)]
    unnamed x6 -> x4, local copies, waits for them, and re-layouts: 1.26 us -> 6.61 us
    pallas_call x1, Pallas kernels: 132 us -> 129 us  [network(): pl.pallas_call(partial(body, lat_total, lon_total), out_shape=(jax.ShapeD...]
    pallas_call x2 -> x0, local copies, waits for them, and re-layouts: 2.74 us -> none  [network(): pl.pallas_call(partial(body, lat_total, lon_total), out_shape=(jax.ShapeD...]
where the time goes in v4:
time: 138 us; the launch traced here: 137 us
  Pallas kernels  129 us (93%)
  local copies, waits for them, and re-layouts  6.61 us (5%)
    pallas_call x1, Pallas kernels, network(): pl.pallas_call(partial(body, lat_total, lon_total), out_shape=(jax.ShapeD...  129 us
    unnamed x4, local copies, waits for them, and re-layouts  6.61 us

profile of v4, /device:TPU:8, one launch (start us, length us, event | category | flops | bytes accessed | tf_op | source)
XLA Modules:
  0.0 137.3 jit_solution(17431775491160610466)
XLA Ops:
  1.3 129.4 %network.1 = (bf16[12,6,4,512]{3,2,1,0:T(4,128)(2,1)}, f32[12,6,4,512]{3,2,1,0:T(4,128)}, f32[2,8,1536]{2,1,0:T(8,128)}, f32[2,8,512]{2,1,0:T(8,128)}) custom-call(bf16[12,6,4,512]{3,2,1,0:T(4,128)(2,1)} %bitcast.15, bf16[12,6,4,512]{3,2,1,0:T(4,128)(2,1)} %bitcast.16, s32[1]{0:T(128)S(6)} %copy.13.depth_ref, bf16[2,512,1536]{2,1,0:T(8,128)(2,1)} %bitcast.12, ...), custom_call_target="tpu_custom_call" | custom-call | tf_op jit(solution)/shard_map/network/pallas_call | solution.py:775
  130.7 1.8 %copy.14 = bf16[1,4,12,6,512]{4,1,3,2,0:T(4,128)(2,1)} copy(bf16[1,4,12,6,512]{4,1,3,2,0:T(4,128)(2,1)} %bitcast.17) | data formatting | bytes 589824
  132.4 1.9 %copy.15 = f32[1,4,12,6,512]{4,1,3,2,0:T(4,128)} copy(f32[1,4,12,6,512]{4,1,3,2,0:T(4,128)} %bitcast.14) | data formatting | bytes 1179648
  134.3 1.5 %copy.16 = f32[1,2,8,1536]{3,2,1,0:T(8,128)} copy(f32[1,2,8,1536]{3,2,1,0:T(8,128)} %bitcast.18) | data formatting | bytes 196608
  135.9 1.4 %copy.17 = f32[1,2,8,512]{3,2,1,0:T(8,128)} copy(f32[1,2,8,512]{3,2,1,0:T(8,128)} %bitcast.19) | data formatting | bytes 65536

commit v5 on v4

--- a/solution.py
+++ b/solution.py
@@ -527,6 +527,10 @@
         def _():
             weight_term(2)
 
+            @pl.when(first)
+            def _():
+                stage_two(3)
+
         rim_near(sl).wait_recv()
         arrive_far(rim_far(sl))
         pairs_low = jnp.concatenate(
@@ -603,22 +607,20 @@
         for unit in (3, 2, 1, 0):
             for tile in range(2):
                 pair_copy(unit, tile, 0).start()
+        stage_two(3)
 
     hand_over(0, grad_copy(0), grad_in, grads)
-    stage_two(3)
     stage_two(2)
     stage_three(3)
     stage_two(1)
     stage_three(2)
+    stage_two(0)
     stage_four(3)
     stage_three(1)
     stage_four(2)
-    stage_two(0)
+    stage_three(0)
     stage_four(1)
     stage_five(3)
-    stage_five(2)
-    stage_three(0)
-    stage_five(1)
     for pair in range(2):
         came = jnp.logical_not(jnp.logical_and(at_home, high == pair))
 
@@ -632,7 +634,9 @@
         put_rows(out_ref, half, [out_in[pair, index].astype(F32) for pair in range(2)])
         put_rows(grad_ref, half, [grad_in[pair, index] for pair in range(2)])
 
+    stage_five(2)
     stage_four(0)
+    stage_five(1)
     stage_five(0)
 
     piece = D // (lat_total * lon_total)

time: 138 us -> 132 us (0.957)
  Pallas kernels: 129 us -> 123 us
    pallas_call x1, Pallas kernels: 129 us -> 123 us  [network(): pl.pallas_call(partial(body, lat_total, lon_total), out_shape=(jax.ShapeD...]
where the time goes in v5:
time: 132 us; the launch traced here: 131 us
  Pallas kernels  123 us (93%)
  local copies, waits for them, and re-layouts  6.61 us (5%)
    pallas_call x1, Pallas kernels, network(): pl.pallas_call(partial(body, lat_total, lon_total), out_shape=(jax.ShapeD...  123 us
    unnamed x4, local copies, waits for them, and re-layouts  6.61 us

profile of v5, /device:TPU:8, one launch (start us, length us, event | category | flops | bytes accessed | tf_op | source)
XLA Modules:
  0.0 130.8 jit_solution(1301364349930249710)
XLA Ops:
  1.3 122.9 %network.1 = (bf16[12,6,4,512]{3,2,1,0:T(4,128)(2,1)}, f32[12,6,4,512]{3,2,1,0:T(4,128)}, f32[2,8,1536]{2,1,0:T(8,128)}, f32[2,8,512]{2,1,0:T(8,128)}) custom-call(bf16[12,6,4,512]{3,2,1,0:T(4,128)(2,1)} %bitcast.15, bf16[12,6,4,512]{3,2,1,0:T(4,128)(2,1)} %bitcast.16, s32[1]{0:T(128)S(6)} %copy.13.depth_ref, bf16[2,512,1536]{2,1,0:T(8,128)(2,1)} %bitcast.12, ...), custom_call_target="tpu_custom_call" | custom-call | tf_op jit(solution)/shard_map/network/pallas_call | solution.py:779
  124.2 1.8 %copy.14 = bf16[1,4,12,6,512]{4,1,3,2,0:T(4,128)(2,1)} copy(bf16[1,4,12,6,512]{4,1,3,2,0:T(4,128)(2,1)} %bitcast.17) | data formatting | bytes 589824
  126.0 1.9 %copy.15 = f32[1,4,12,6,512]{4,1,3,2,0:T(4,128)} copy(f32[1,4,12,6,512]{4,1,3,2,0:T(4,128)} %bitcast.14) | data formatting | bytes 1179648
  127.9 1.5 %copy.16 = f32[1,2,8,1536]{3,2,1,0:T(8,128)} copy(f32[1,2,8,1536]{3,2,1,0:T(8,128)} %bitcast.18) | data formatting | bytes 196608
  129.4 1.4 %copy.17 = f32[1,2,8,512]{3,2,1,0:T(8,128)} copy(f32[1,2,8,512]{3,2,1,0:T(8,128)} %bitcast.19) | data formatting | bytes 65536

commit v6 on v5

--- a/solution.py
+++ b/solution.py
@@ -463,6 +463,10 @@
         stream = stream + act_s[sl][0:1, 0:1] * dot(mixed_low, wout_s[sl, 1], (1, 0))
         for part in range(2):
             outs[sl, part] = stream[HALF * part : HALF * part + HALF].astype(BF16)
+        @pl.when(jnp.logical_and(first, sl == 1))
+        def _():
+            act_copy.start()
+
         hand_over(sl, out_copy(sl), out_in, outs)
 
         @pl.when(sl == 0)
@@ -483,7 +487,6 @@
 
     @pl.when(first)
     def _():
-        act_copy.start()
         gact_copy.wait_recv()
 
     @pl.when(jnp.logical_not(jnp.logical_or(first, at_home)))
@@ -596,7 +599,10 @@
 
             g_s[...] = g + rows_of(gin, 1)
 
-        weight_term(2 * sl + 1)
+        @pl.when(jnp.logical_or(first, step == 1))
+        def _():
+            weight_term(2 * sl + 1)
+
         return carry
 
     lax.fori_loop(0, 2, backward, 0)
@@ -604,6 +610,7 @@
 
     @pl.when(jnp.logical_not(first))
     def _():
+        weight_term(3)
         for unit in (3, 2, 1, 0):
             for tile in range(2):
                 pair_copy(unit, tile, 0).start()
@@ -794,11 +801,29 @@
     )(fields, cotangent, depths, w_qkv, w_out)
 
 
+def copier(*refs):
+    count = len(refs) // 2
+    for source, target in zip(refs[:count], refs[count:]):
+        target[...] = source[...]
+
+
+def copied(*arrays):
+    vmem = pl.BlockSpec(memory_space=pltpu.VMEM)
+    return pl.pallas_call(
+        copier,
+        out_shape=tuple(jax.ShapeDtypeStruct(a.shape, a.dtype) for a in arrays),
+        in_specs=[vmem] * len(arrays),
+        out_specs=(vmem,) * len(arrays),
+        name="copied",
+    )(*arrays)
+
+
 def local(fields, cotangent, depths, w_qkv, w_out):
     out_rows, grad_rows, qkv_grad, out_grad = network(
         fields.transpose(1, 2, 0, 3), cotangent.transpose(1, 2, 0, 3), depths, w_qkv[0], w_out[0],
         lax.axis_size("lat"), lax.axis_size("lon"),
     )
+    out_rows, grad_rows, qkv_grad, out_grad = copied(out_rows, grad_rows, qkv_grad, out_grad)
     return (
         out_rows.transpose(2, 0, 1, 3)[None],
         grad_rows.transpose(2, 0, 1, 3)[None],

time: 132 us -> 126 us (0.955)
  local copies, waits for them, and re-layouts: 6.61 us -> 0 us
    unnamed x4 -> x0, local copies, waits for them, and re-layouts: 6.61 us -> none
    pallas_call x0 -> x1, Pallas kernels: none -> 2.14 us  [copied(): pl.pallas_call(copier, out_shape=tuple((jax.ShapeDtypeStruct(a.shape, a.d...]
    pallas_call x1, Pallas kernels: 123 us -> 121 us  [network(): pl.pallas_call(partial(body, lat_total, lon_total), out_shape=(jax.ShapeD...]
where the time goes in v6:
time: 126 us; the launch traced here: 125 us
  Pallas kernels  123 us (98%)
  between operations  1.29 us (1%)
    pallas_call x1, Pallas kernels, network(): pl.pallas_call(partial(body, lat_total, lon_total), out_shape=(jax.ShapeD...  121 us

profile of v6, /device:TPU:8, one launch (start us, length us, event | category | flops | bytes accessed | tf_op | source)
XLA Modules:
  0.0 124.7 jit_solution(18292126495040959288)
XLA Ops:
  1.3 121.3 %network.1 = (bf16[12,6,4,512]{3,2,1,0:T(4,128)(2,1)}, f32[12,6,4,512]{3,2,1,0:T(4,128)}, f32[2,8,1536]{2,1,0:T(8,128)}, f32[2,8,512]{2,1,0:T(8,128)}) custom-call(bf16[12,6,4,512]{3,2,1,0:T(4,128)(2,1)} %bitcast.14, bf16[12,6,4,512]{3,2,1,0:T(4,128)(2,1)} %bitcast.15, s32[1]{0:T(128)S(6)} %copy.9.depth_ref, bf16[2,512,1536]{2,1,0:T(8,128)(2,1)} %bitcast.12, ...), custom_call_target="tpu_custom_call" | custom-call | tf_op jit(solution)/shard_map/network/pallas_call | solution.py:786
  122.6 2.1 %copied.1 = (bf16[12,6,4,512]{3,2,1,0:T(4,128)(2,1)}, f32[12,6,4,512]{3,2,1,0:T(4,128)}, f32[2,8,1536]{2,1,0:T(8,128)}, f32[2,8,512]{2,1,0:T(8,128)}) custom-call(bf16[12,6,4,512]{3,2,1,0:T(4,128)(2,1)} %get-tuple-element.12.refs_0_, f32[12,6,4,512]{3,2,1,0:T(4,128)} %get-tuple-element.13.refs_1_, f32[2,8,1536]{2,1,0:T(8,128)} %get-tuple-element.14.refs_2_, ...), custom_call_target="tpu_custom_call" | custom-call | tf_op jit(solution)/shard_map/copied/pallas_call | solution.py:812
